TPU v7x, 128 devices: a whole 4x4x4 slice. The times are simulated.
128 devices in a mesh: section: 4 (over z), dp: 32 (over x, y, core).
Axes of the slice: x: 4, y: 4, z: 4, core: 2. Of those that a mesh axis runs over, the one named last changes fastest.
Arguments:
- block_input: bfloat16 [128, 128, 1024], P('dp'), may hold values from -6 to 6
- cotangent: bfloat16 [128, 128, 1024], P('dp'), may hold values from -6 to 6
- group_ids: int32 [128], P('dp'), may hold values from 0 to 7
- live_count: int32 [32], P('dp'), may hold values from 1 to 4, as said below
- group_scale: float32 [8], replicated, may hold values from 0.25 to 4
- norm_gain: float32 [4, 2, 1024], P('section'), may hold values from 0.1 to 1.9
- norm_bias: float32 [4, 2, 1024], P('section'), may hold values from -2 to 2
- first_weight: bfloat16 [4, 1024, 4096], P('section'), may hold values from -0.1875 to 0.1875
- qv_bias: float32 [2, 2, 1024], replicated, may hold values from -2 to 2
- up_bias: float32 [2, 4096], replicated, may hold values from -2 to 2
- down_weight: bfloat16 [8192, 1024], P('section'), may hold values from -0.09375 to 0.09375
- out_bias: float32 [4, 1024], P('section'), may hold values from -2 to 2
Outputs:
- input_grad: bfloat16 [128, 128, 1024], P('dp', None, 'section')
- first_grad: float32 [4, 1024, 4096], P('section')
- down_grad: float32 [8192, 1024], P('section')
- qv_bias_grad: float32 [2, 2, 1024], replicated
- up_bias_grad: float32 [2, 4096], replicated
- out_bias_grad: float32 [4, 1024], P('section')
- norm_gain_grad: float32 [4, 2, 1024], P('section')
- norm_bias_grad: float32 [4, 2, 1024], P('section')
Inputs may be any that keep to these rules, and one draw needn't show every extreme that they name: `live_count`: live slots of each index of dp, counted from its first slot; the slots after them hold sequences of weight zero; some index of dp has all 4 live and some has one.
All inputs are finite; a program needn't handle non-finite values.
Results may differ from a plain program's by a relative error of at most 0.023.
Values may be sent and summed in bfloat16 or wider, within the bound.
A program may use at most 256 MiB of HBM per device.

v0:
```python
from functools import partial
import math

import jax
import jax.numpy as jnp
from jax import lax
from jax.sharding import PartitionSpec as P

HEADS = 16
MICRO = 4


relax_alpha = 32.0
norm_eps = 1e-05
far_below = -1000000000.0


def passed_along(value, axis, steps):
    count = lax.axis_size(axis)
    initial, last = (max(0, -steps), min(count, count - steps))
    return lax.ppermute(value, axis, [(source, source + steps) for source in range(initial, last)])


def normalize(entries):
    average = jnp.mean(entries, axis=-1, keepdims=True)
    centered = entries - average
    inverse = lax.rsqrt(jnp.mean(centered * centered, axis=-1, keepdims=True) + norm_eps)
    return (centered * inverse, inverse)


def norm_backward(grad_out, normalized, inverse, gain_row):
    scaled = grad_out * gain_row
    middle = jnp.mean(scaled, axis=-1, keepdims=True)
    along = jnp.mean(scaled * normalized, axis=-1, keepdims=True)
    return inverse * (scaled - middle - normalized * along)


def contract_rows(left_side, right_side):
    return lax.dot_general(
        left_side, right_side, (((0,), (0,)), ((), ())), preferred_element_type=jnp.float32
    )


def contract_columns(left_side, right_side):
    return lax.dot_general(
        left_side, right_side, (((1,), (1,)), ((), ())), preferred_element_type=jnp.float32
    )


def take_slot(buffer, position):
    return lax.dynamic_index_in_dim(buffer, position, 0, keepdims=False)


def place_slot(buffer, position, entries, running):
    previous = take_slot(buffer, position)
    return lax.dynamic_update_index_in_dim(
        buffer, jnp.where(running, entries, previous), position, 0
    )


def causal_scores(query_heads, key_heads):
    length = query_heads.shape[1]
    score_scale = 1.0 / (relax_alpha * math.sqrt(query_heads.shape[-1]))
    scores = (
        jnp.einsum("sqhd,skhd->shqk", query_heads, key_heads, preferred_element_type=jnp.float32)
        * score_scale
    )
    row_index = lax.broadcasted_iota(jnp.int32, (length, length), 0)
    column_index = lax.broadcasted_iota(jnp.int32, (length, length), 1)
    return jnp.where(row_index >= column_index, scores, far_below)


def on_device(
    block_input,
    cotangent,
    group_ids,
    live_count,
    group_scale,
    norm_gain,
    norm_bias,
    first_weight,
    qv_bias,
    up_bias,
    down_weight,
    out_bias,
):
    slot_count, length, model_width = block_input.shape
    hidden_width = first_weight.shape[2]
    micro_count = MICRO
    micro_sequences = slot_count // micro_count
    row_count = micro_sequences * length
    head_count = HEADS
    head_size = model_width // head_count
    section_at = lax.axis_index("section")
    sections = lax.axis_size("section")
    attending = section_at % 2 == 0
    layer_at = section_at // 2
    weight = first_weight[0]
    gain_pair = norm_gain[0]
    shift_pair = norm_bias[0]
    branch_bias = out_bias[0]
    bias_pair = take_slot(qv_bias, layer_at)
    hidden_bias = take_slot(up_bias, layer_at)
    partner_down = passed_along(down_weight, "section", 1)
    full_down = jnp.concatenate([partner_down, down_weight], axis=0)
    labels = jnp.arange(group_scale.shape[0], dtype=jnp.int32)
    chosen = jnp.sum(
        jnp.where(group_ids[:, None] == labels[None, :], group_scale[None, :], 0.0), axis=1
    )
    alive_slots = jnp.arange(slot_count, dtype=jnp.int32) < live_count[0]
    sequence_weight = jnp.where(alive_slots, chosen, 0.0)
    weighted = cotangent.astype(jnp.float32) * sequence_weight[:, None, None]

    def project_inputs(normed):
        bias_row = jnp.concatenate([bias_pair[0], jnp.zeros_like(bias_pair[0]), bias_pair[1]])
        projected = (
            jnp.dot(normed, weight[:, : 3 * model_width], preferred_element_type=jnp.float32)
            + bias_row
        )
        return projected.astype(jnp.bfloat16)

    def split_three(projected):
        return tuple(
            (
                projected[:, column_block * model_width : (column_block + 1) * model_width].reshape(
                    micro_sequences, length, head_count, head_size
                )
                for column_block in range(3)
            )
        )

    def attention_forward(normed):
        query_heads, key_heads, value_heads = split_three(project_inputs(normed))
        logits = relax_alpha * causal_scores(query_heads, key_heads)
        row_top = jnp.max(logits, axis=-1, keepdims=True)
        powers = jnp.exp(logits - row_top)
        row_total = jnp.sum(powers, axis=-1, keepdims=True)
        weights_low = (powers / row_total).astype(jnp.bfloat16)
        context = jnp.einsum(
            "shqk,skhd->sqhd", weights_low, value_heads, preferred_element_type=jnp.float32
        )
        context = context.reshape(row_count, model_width).astype(jnp.bfloat16)
        branch = contract_columns(context, weight[:, 3 * model_width :]) + branch_bias
        log_total = (row_top + jnp.log(row_total))[..., 0]
        return (branch, jnp.zeros((row_count, hidden_width), jnp.float32), log_total)

    def feed_forward(normed):
        hidden = jnp.dot(normed, weight, preferred_element_type=jnp.float32) + hidden_bias
        active = jax.nn.gelu(hidden, approximate=True).astype(jnp.bfloat16)
        branch = jnp.dot(active, full_down, preferred_element_type=jnp.float32) + branch_bias
        return (branch, hidden, jnp.zeros((micro_sequences, head_count, length), jnp.float32))

    def forward_step(residual):
        residual_wide = residual.astype(jnp.float32)
        unit_pre, inverse_pre = normalize(residual_wide)
        normed = (unit_pre * gain_pair[0] + shift_pair[0]).astype(jnp.bfloat16)
        branch, hidden, log_total = lax.cond(attending, attention_forward, feed_forward, normed)
        unit_post, inverse_post = normalize(branch)
        output = residual_wide + unit_post * gain_pair[1] + shift_pair[1]
        return (output, normed, branch, hidden, log_total)

    def forward_spare(residual):
        return (
            jnp.zeros((row_count, model_width), jnp.float32),
            jnp.zeros((row_count, model_width), jnp.bfloat16),
            jnp.zeros((row_count, model_width), jnp.float32),
            jnp.zeros((row_count, hidden_width), jnp.float32),
            jnp.zeros((micro_sequences, head_count, length), jnp.float32),
        )

    store_input = jnp.zeros((micro_count, row_count, model_width), jnp.bfloat16)
    store_normed = jnp.zeros((micro_count, row_count, model_width), jnp.bfloat16)
    store_branch = jnp.zeros((micro_count, row_count, model_width), jnp.float32)
    store_hidden = jnp.zeros((micro_count, row_count, hidden_width), jnp.float32)
    store_total = jnp.zeros((micro_count, micro_sequences, head_count, length), jnp.float32)
    arriving = jnp.zeros((row_count, model_width), jnp.bfloat16)
    steps_total = micro_count + sections - 1
    for step_at in range(steps_total):
        micro_at = step_at - section_at
        running = (micro_at >= 0) & (micro_at < micro_count)
        clipped = jnp.clip(micro_at, 0, micro_count - 1)
        residual = jnp.where(section_at == 0, take_slot(block_input, clipped), arriving)
        output, normed, branch, hidden, log_total = lax.cond(
            running, forward_step, forward_spare, residual
        )
        store_input = place_slot(store_input, clipped, residual, running)
        store_normed = place_slot(store_normed, clipped, normed, running)
        store_branch = place_slot(store_branch, clipped, branch, running)
        store_hidden = place_slot(store_hidden, clipped, hidden, running)
        store_total = place_slot(store_total, clipped, log_total, running)
        if step_at + 1 < steps_total:
            arriving = passed_along(output.astype(jnp.bfloat16), "section", 1)

    def attention_backward(operands):
        grad_branch, normed, hidden, log_total, first_sum, down_sum, pair_sum, hidden_sum = operands
        query_heads, key_heads, value_heads = split_three(project_inputs(normed))
        logits = relax_alpha * causal_scores(query_heads, key_heads)
        attention_weights = jnp.exp(logits - log_total[..., None])
        weights_low = attention_weights.astype(jnp.bfloat16)
        context = jnp.einsum(
            "shqk,skhd->sqhd", weights_low, value_heads, preferred_element_type=jnp.float32
        )
        context = context.reshape(row_count, model_width).astype(jnp.bfloat16)
        output_part = contract_rows(grad_branch, context)
        grad_context = jnp.dot(
            grad_branch, weight[:, 3 * model_width :], preferred_element_type=jnp.float32
        ).astype(jnp.bfloat16)
        grad_heads = grad_context.reshape(micro_sequences, length, head_count, head_size)
        grad_value = jnp.einsum(
            "shqk,sqhd->skhd", weights_low, grad_heads, preferred_element_type=jnp.float32
        )
        grad_weights = jnp.einsum(
            "sqhd,skhd->shqk", grad_heads, value_heads, preferred_element_type=jnp.float32
        )
        grad_logits = attention_weights * (
            grad_weights - jnp.sum(attention_weights * grad_weights, axis=-1, keepdims=True)
        )
        grad_scores = (relax_alpha * grad_logits).astype(jnp.bfloat16)
        score_scale = 1.0 / (relax_alpha * math.sqrt(head_size))
        grad_query = (
            jnp.einsum(
                "shqk,skhd->sqhd", grad_scores, key_heads, preferred_element_type=jnp.float32
            )
            * score_scale
        )
        grad_key = (
            jnp.einsum(
                "shqk,sqhd->skhd", grad_scores, query_heads, preferred_element_type=jnp.float32
            )
            * score_scale
        )
        grad_projected = jnp.concatenate(
            [
                grad_part.reshape(row_count, model_width)
                for grad_part in (grad_query, grad_key, grad_value)
            ],
            axis=1,
        ).astype(jnp.bfloat16)
        first_sum = first_sum.at[:, : 3 * model_width].add(contract_rows(normed, grad_projected))
        first_sum = first_sum.at[:, 3 * model_width :].add(output_part)
        column_sums = jnp.sum(grad_projected.astype(jnp.float32), axis=0)
        pair_sum = pair_sum + jnp.stack([column_sums[:model_width], column_sums[2 * model_width :]])
        grad_normed = contract_columns(grad_projected, weight[:, : 3 * model_width])
        return (grad_normed, first_sum, down_sum, pair_sum, hidden_sum)

    def feed_backward(operands):
        grad_branch, normed, hidden, log_total, first_sum, down_sum, pair_sum, hidden_sum = operands
        active, gelu_back = jax.vjp(partial(jax.nn.gelu, approximate=True), hidden)
        down_sum = down_sum + contract_rows(active.astype(jnp.bfloat16), grad_branch)
        grad_active = contract_columns(grad_branch, full_down)
        grad_hidden = gelu_back(grad_active)[0].astype(jnp.bfloat16)
        first_sum = first_sum + contract_rows(normed, grad_hidden)
        hidden_sum = hidden_sum + jnp.sum(grad_hidden.astype(jnp.float32), axis=0)
        grad_normed = contract_columns(grad_hidden, weight)
        return (grad_normed, first_sum, down_sum, pair_sum, hidden_sum)

    def backward_run(operands):
        carried, clipped, incoming = operands
        first_sum, down_sum, pair_sum, hidden_sum, branch_sum, gain_sum, shift_sum = carried
        residual_wide = take_slot(store_input, clipped).astype(jnp.float32)
        normed = take_slot(store_normed, clipped)
        branch = take_slot(store_branch, clipped)
        unit_post, inverse_post = normalize(branch)
        gain_post = jnp.sum(incoming * unit_post, axis=0)
        shift_post = jnp.sum(incoming, axis=0)
        grad_branch = norm_backward(incoming, unit_post, inverse_post, gain_pair[1]).astype(
            jnp.bfloat16
        )
        branch_sum = branch_sum + jnp.sum(grad_branch.astype(jnp.float32), axis=0)
        grad_normed, first_sum, down_sum, pair_sum, hidden_sum = lax.cond(
            attending,
            attention_backward,
            feed_backward,
            (
                grad_branch,
                normed,
                take_slot(store_hidden, clipped),
                take_slot(store_total, clipped),
                first_sum,
                down_sum,
                pair_sum,
                hidden_sum,
            ),
        )
        unit_pre, inverse_pre = normalize(residual_wide)
        gain_pre = jnp.sum(grad_normed * unit_pre, axis=0)
        shift_pre = jnp.sum(grad_normed, axis=0)
        grad_residual = incoming + norm_backward(grad_normed, unit_pre, inverse_pre, gain_pair[0])
        gain_sum = gain_sum + jnp.stack([gain_pre, gain_post])
        shift_sum = shift_sum + jnp.stack([shift_pre, shift_post])
        return (
            grad_residual,
            (first_sum, down_sum, pair_sum, hidden_sum, branch_sum, gain_sum, shift_sum),
        )

    def backward_spare(operands):
        carried, clipped, incoming = operands
        return (jnp.zeros((row_count, model_width), jnp.float32), carried)

    carried = (
        jnp.zeros((model_width, hidden_width), jnp.float32),
        jnp.zeros((hidden_width, model_width), jnp.float32),
        jnp.zeros((2, model_width), jnp.float32),
        jnp.zeros((hidden_width,), jnp.float32),
        jnp.zeros((model_width,), jnp.float32),
        jnp.zeros((2, model_width), jnp.float32),
        jnp.zeros((2, model_width), jnp.float32),
    )
    input_grads = jnp.zeros((micro_count, row_count, model_width), jnp.float32)
    arriving_grad = jnp.zeros((row_count, model_width), jnp.bfloat16)
    for step_at in range(steps_total):
        micro_at = step_at - (sections - 1 - section_at)
        running = (micro_at >= 0) & (micro_at < micro_count)
        clipped = jnp.clip(micro_at, 0, micro_count - 1)
        incoming = jnp.where(
            section_at == sections - 1,
            take_slot(weighted, clipped),
            arriving_grad.astype(jnp.float32),
        )
        grad_residual, carried = lax.cond(
            running, backward_run, backward_spare, (carried, clipped, incoming)
        )
        input_grads = place_slot(input_grads, clipped, grad_residual, running & (section_at == 0))
        if step_at + 1 < steps_total:
            arriving_grad = passed_along(grad_residual.astype(jnp.bfloat16), "section", -1)
    spread = lax.psum_scatter(
        input_grads.astype(jnp.bfloat16), "section", scatter_dimension=2, tiled=True
    )
    first_sum, down_sum, pair_sum, hidden_sum, branch_sum, gain_sum, shift_sum = carried
    layer_mask = (jnp.arange(qv_bias.shape[0], dtype=jnp.int32) == layer_at).astype(jnp.float32)
    attend_mask = layer_mask * attending.astype(jnp.float32)
    feed_mask = layer_mask * (1.0 - attending.astype(jnp.float32))
    pair_full = attend_mask[:, None, None] * pair_sum[None]
    hidden_full = feed_mask[:, None] * hidden_sum[None]
    pair_total, hidden_total = lax.psum((pair_full, hidden_full), ("section", "dp"))
    half_rows = down_sum.shape[0] // 2
    first_total, down_reduced, branch_total, gain_total, shift_total = (
        lax.psum(first_sum.astype(jnp.bfloat16), "dp").astype(jnp.float32),
        lax.psum(down_sum.astype(jnp.bfloat16), "dp").astype(jnp.float32),
        lax.psum(branch_sum.astype(jnp.bfloat16), "dp").astype(jnp.float32),
        lax.psum(gain_sum.astype(jnp.bfloat16), "dp").astype(jnp.float32),
        lax.psum(shift_sum.astype(jnp.bfloat16), "dp").astype(jnp.float32),
    )
    partner_rows = passed_along(
        down_reduced[:half_rows].astype(jnp.bfloat16), "section", -1
    ).astype(jnp.float32)
    down_total = jnp.where(attending, partner_rows, down_reduced[half_rows:])
    return (
        spread,
        first_total[None],
        down_total,
        pair_total,
        hidden_total,
        branch_total[None],
        gain_total[None],
        shift_total[None],
    )


def solution(mesh):
    in_specs = (
        P("dp", None, None),
        P("dp", None, None),
        P("dp"),
        P("dp"),
        P(),
        P("section", None, None),
        P("section", None, None),
        P("section", None, None),
        P(),
        P(),
        P("section", None),
        P("section", None),
    )
    out_specs = (
        P("dp", None, "section"),
        P("section", None, None),
        P("section", None),
        P(),
        P(),
        P("section", None),
        P("section", None, None),
        P("section", None, None),
    )
    return jax.shard_map(
        on_device, mesh=mesh, in_specs=in_specs, out_specs=out_specs, check_vma=False
    )
```

profile of v0, /device:TPU:33, one launch (start us, length us, event | category | flops | bytes accessed | tf_op | source)
XLA Modules:
  0.0 1243.9 jit_solution(4680480584489310492)
XLA Ops:
  17.7 84.2 %collective-permute-done = bf16[2048,1024]{1,0:T(8,128)(2,1)} collective-permute-done((bf16[2048,1024]{1,0:T(8,128)(2,1)}, bf16[2048,1024]{1,0:T(8,128)(2,1)}, u32[]{:S(2)}, u32[]{:S(2)}) %collective-permute-start) | collective-permute-done | bytes 4194336 | tf_op jit(solution)/shard_map/ppermute | solution.py:21
  101.9 4.6 constant_dynamic-update-slice_fusion.8
  120.8 8.6 collective-permute-done.1
  131.2 17.4 %conditional.29 = (f32[128,1024]{1,0:T(8,128)S(1)}, bf16[128,1024]{1,0:T(8,128)(2,1)}, f32[128,1024]{1,0:T(8,128)}, f32[128,4096]{1,0:T(8,128)}, f32[1,16,128]{2,1,0:T(8,128)}) conditional(s32[]{:T(128)} %convert_element_type.928, () %tuple.393, (bf16[128,1024]{1,0:T(8,128)(2,1)S(1)}, pred[]{:T(512)}, f32[2,1024]{1,0:T(2,128)S(1)}, ...), branch_computations={%region_10.11_spmd, %region_11.20_spmd} | conditional | flops 2155741440 | bytes 28005560 | solution.py:183
  132.5 12.4 conditional.1
  132.7 6.1 convolution_add_fusion.1
  138.8 5.6 fusion.46
  167.4 16.9 %conditional.30 = (f32[128,1024]{1,0:T(8,128)S(1)}, bf16[128,1024]{1,0:T(8,128)(2,1)}, f32[128,1024]{1,0:T(8,128)}, f32[128,4096]{1,0:T(8,128)}, f32[1,16,128]{2,1,0:T(8,128)}) conditional(s32[]{:T(128)} %convert_element_type.930, () %tuple.395, (bf16[128,1024]{1,0:T(8,128)(2,1)S(1)}, pred[]{:T(512)}, f32[2,1024]{1,0:T(2,128)S(1)}, ...), branch_computations={%region_20.21_spmd, %region_21.30_spmd} | conditional | flops 2155741440 | bytes 28005560 | solution.py:183
  168.8 12.2 conditional.2
  168.8 6.1 convolution_add_fusion.2
  174.8 5.6 fusion.84
  199.1 6.2 collective-permute-done.3
  206.4 29.3 %conditional.31 = (f32[128,1024]{1,0:T(8,128)S(1)}, bf16[128,1024]{1,0:T(8,128)(2,1)}, f32[128,1024]{1,0:T(8,128)}, f32[128,4096]{1,0:T(8,128)}, f32[1,16,128]{2,1,0:T(8,128)}) conditional(s32[]{:T(128)} %convert_element_type.932, () %tuple.397, (bf16[128,1024]{1,0:T(8,128)(2,1)S(1)}, pred[]{:T(512)}, f32[2,1024]{1,0:T(2,128)S(1)}, ...), branch_computations={%region_30.31_spmd, %region_31.40_spmd} | conditional | flops 2155741440 | bytes 28005560 | solution.py:183
  207.7 24.6 %conditional.3 = (f32[128,4096]{1,0:T(8,128)}, f32[1,16,128]{2,1,0:T(8,128)}, f32[128,1024]{1,0:T(8,128)S(1)}, f32[1,1024]{1,0:T(1,128)S(1)}) conditional(s32[]{:T(128)} %convert_element_type.732, (bf16[128,1024]{1,0:T(8,128)(2,1)}, bf16[1024,4096]{1,0:T(8,128)(2,1)}, f32[4096]{0:T(1024)S(1)}, bf16[4096,1024]{1,0:T(8,128)(2,1)}, ...), branch_computations={%region_34.34_spmd, %region_35.37_spmd} | conditional | flops 2152726528 | bytes 24010820 | solution.py:157
  207.7 6.1 convolution_add_fusion.3
  213.8 5.6 fusion.122
  250.4 6.2 collective-permute-done.4
  257.7 16.9 %conditional.32 = (f32[128,1024]{1,0:T(8,128)S(1)}, bf16[128,1024]{1,0:T(8,128)(2,1)}, f32[128,1024]{1,0:T(8,128)}, f32[128,4096]{1,0:T(8,128)}, f32[1,16,128]{2,1,0:T(8,128)}) conditional(s32[]{:T(128)} %convert_element_type.934, () %tuple.399, (bf16[128,1024]{1,0:T(8,128)(2,1)S(1)}, pred[]{:T(512)}, f32[2,1024]{1,0:T(2,128)S(1)}, ...), branch_computations={%region_40.41_spmd, %region_41.50_spmd} | conditional | flops 2155741440 | bytes 28005560 | solution.py:183
  259.1 12.2 conditional.4
  259.1 6.1 convolution_add_fusion.4
  265.1 5.6 fusion.160
  290.5 4.2 conditional.33
  294.8 20.3 %collective-permute-start.6 = (bf16[128,1024]{1,0:T(8,128)(2,1)S(1)}, bf16[128,1024]{1,0:T(8,128)(2,1)S(1)}, u32[]{:S(2)}, u32[]{:S(2)}) collective-permute-start(bf16[128,1024]{1,0:T(8,128)(2,1)S(1)} %convert_element_type.937), channel_id=1, source_target_pairs={{0,32},{32,64},{64,96},{1,33},{33,65},{65,97},{2,34},{34,66},{66,9... | collective-permute-start | bytes 786440 | tf_op jit(solution)/shard_map/ppermute | solution.py:21
  334.7 25.2 %conditional.35 = (f32[128,1024]{1,0:T(8,128)S(1)}, f32[1024,4096]{0,1:T(8,128)}, f32[4096,1024]{1,0:T(8,128)}, f32[2,1024]{1,0:T(2,128)}, f32[4096]{0:T(1024)},...) conditional(s32[]{:T(128)} %convert_element_type.924, () %tuple.390, (pred[]{:T(512)}, ...), branch_computations={%region_69.70_spmd, %region_70.90_spmd} | conditional | flops 4317637632 | bytes 126373392 | solution.py:320
  334.7 8.3 broadcast_in_dim.346
  343.0 7.9 broadcast_in_dim.347
  363.4 7.3 collective-permute-done.7
  371.5 8.8 conditional.36
  384.1 80.0 %collective-permute-done.8 = bf16[128,1024]{1,0:T(8,128)(2,1)S(1)} collective-permute-done((bf16[128,1024]{1,0:T(8,128)(2,1)}, bf16[128,1024]{1,0:T(8,128)(2,1)S(1)}, u32[]{:S(2)}, u32[]{:S(2)}) %collective-permute-start.8) | collective-permute-done | bytes 262176 | tf_op jit(solution)/shard_map/ppermute | solution.py:21
  464.9 53.8 %conditional.37 = (f32[128,1024]{1,0:T(8,128)}, f32[1024,4096]{0,1:T(8,128)}, f32[4096,1024]{1,0:T(8,128)}, f32[2,1024]{1,0:T(2,128)}, f32[4096]{0:T(1024)}, /*i...) conditional(s32[]{:T(128)} %convert_element_type.942, (f32[1024,4096]{0,1:T(8,128)}, ...), branch_computations={%region_111.112_spmd, %region_112.132_spmd} | conditional | flops 4326035456 | bytes 134418288 | solution.py:320
  469.7 41.0 %conditional.9 = (f32[128,1024]{1,0:T(8,128)S(1)}, f32[1024,4096]{0,1:T(8,128)}, f32[4096,1024]{1,0:T(8,128)}, f32[2,1024]{1,0:T(2,128)}, f32[4096]{0:T(1024)}) conditional(s32[]{:T(128)} %convert_element_type.812, (bf16[128,1024]{1,0:T(8,128)(2,1)S(1)}, bf16[4096,1024]{1,0:T(8,128)(2,1)}, f32[4,128,4096]{2,1,0:T(8,128)}, s32[]{:T(128)}, ...), branch_computations={%region_119.120_spmd, %region_121.124_spmd} | conditional | flops 4319608832 | bytes 126157384 | solution.py:270
  469.8 7.8 convert_reduce_fusion.15
  480.4 14.3 %bitcast_add_fusion.1 = f32[1024,4096]{0,1:T(8,128)} fusion(f32[1024,4096]{0,1:T(8,128)} %get-tuple-element.2523, bf16[128,4096]{1,0:T(8,128)(2,1)S(1)} %get-tuple-element.3052, bf16[128,1024]{1,0:T(8,128)(2,1)S(1)} %get-tuple-element.2524), kind=kOutput, calls=%fused_computation.570 | convolution fusion | flops 1077936128 | bytes 34865152 | tf_op jit(solution)/shard_map/cond/branch_1_fun/cond/branch_0_fun/dot_general | solution.py:39
  494.7 14.5 %convolution_add_fusion.9 = f32[4096,1024]{1,0:T(8,128)} fusion(f32[4096,1024]{1,0:T(8,128)} %get-tuple-element.2525, bf16[128,1024]{1,0:T(8,128)(2,1)S(1)} %get-tuple-element.2518, f32[4,128,4096]{2,1,0:T(8,128)} %get-tuple-element.2520, s32[]{:T(128)} %get-tuple-element.2521), kind=kOutput, calls=%fused_computation.571 | convolution fusion | flops 1082654720 | bytes 35914240 | tf_op jit(solution)/shard_map/cond/branch_1_fun/cond/branch_0_fun/dot_general | solution.py:39
  522.3 12.8 %collective-permute-done.9 = bf16[128,1024]{1,0:T(8,128)(2,1)S(1)} collective-permute-done((bf16[128,1024]{1,0:T(8,128)(2,1)}, bf16[128,1024]{1,0:T(8,128)(2,1)S(1)}, u32[]{:S(2)}, u32[]{:S(2)}) %collective-permute-start.9) | collective-permute-done | bytes 262176 | tf_op jit(solution)/shard_map/ppermute | solution.py:21
  536.0 48.6 %conditional.38 = (f32[128,1024]{1,0:T(8,128)}, f32[1024,4096]{0,1:T(8,128)}, f32[4096,1024]{1,0:T(8,128)}, f32[2,1024]{1,0:T(2,128)}, f32[4096]{0:T(1024)}, /*i...) conditional(s32[]{:T(128)} %convert_element_type.945, (f32[1024,4096]{0,1:T(8,128)}, ...), branch_computations={%region_132.133_spmd, %region_133.153_spmd} | conditional | flops 4326035456 | bytes 134418288 | solution.py:320
  540.9 41.0 %conditional.10 = (f32[128,1024]{1,0:T(8,128)S(1)}, f32[1024,4096]{0,1:T(8,128)}, f32[4096,1024]{1,0:T(8,128)}, f32[2,1024]{1,0:T(2,128)}, f32[4096]{0:T(1024)}) conditional(s32[]{:T(128)} %convert_element_type.829, (bf16[128,1024]{1,0:T(8,128)(2,1)S(1)}, bf16[4096,1024]{1,0:T(8,128)(2,1)}, f32[4,128,4096]{2,1,0:T(8,128)}, s32[]{:T(128)}, ...), branch_computations={%region_140.141_spmd, %region_142.145_spmd} | conditional | flops 4319608832 | bytes 126157384 | solution.py:270
  540.9 7.8 convert_reduce_fusion.19
  551.6 14.3 %bitcast_add_fusion.2 = f32[1024,4096]{0,1:T(8,128)} fusion(f32[1024,4096]{0,1:T(8,128)} %get-tuple-element.2576, bf16[128,4096]{1,0:T(8,128)(2,1)S(1)} %get-tuple-element.3057, bf16[128,1024]{1,0:T(8,128)(2,1)S(1)} %get-tuple-element.2577), kind=kOutput, calls=%fused_computation.679 | convolution fusion | flops 1077936128 | bytes 34865152 | tf_op jit(solution)/shard_map/cond/branch_1_fun/cond/branch_0_fun/dot_general | solution.py:39
  565.9 14.5 %convolution_add_fusion.10 = f32[4096,1024]{1,0:T(8,128)} fusion(f32[4096,1024]{1,0:T(8,128)} %get-tuple-element.2578, bf16[128,1024]{1,0:T(8,128)(2,1)S(1)} %get-tuple-element.2571, f32[4,128,4096]{2,1,0:T(8,128)} %get-tuple-element.2573, s32[]{:T(128)} %get-tuple-element.2574), kind=kOutput, calls=%fused_computation.680 | convolution fusion | flops 1082654720 | bytes 35914240 | tf_op jit(solution)/shard_map/cond/branch_1_fun/cond/branch_0_fun/dot_general | solution.py:39
  586.4 6.8 collective-permute-start.10
  593.2 12.8 %collective-permute-done.10 = bf16[128,1024]{1,0:T(8,128)(2,1)S(1)} collective-permute-done((bf16[128,1024]{1,0:T(8,128)(2,1)}, bf16[128,1024]{1,0:T(8,128)(2,1)S(1)}, u32[]{:S(2)}, u32[]{:S(2)}) %collective-permute-start.10) | collective-permute-done | bytes 262176 | tf_op jit(solution)/shard_map/ppermute | solution.py:21
  606.9 54.0 %conditional.39 = (f32[128,1024]{1,0:T(8,128)}, f32[1024,4096]{0,1:T(8,128)}, f32[4096,1024]{1,0:T(8,128)}, f32[2,1024]{1,0:T(2,128)}, f32[4096]{0:T(1024)}, /*i...) conditional(s32[]{:T(128)} %convert_element_type.948, (f32[1024,4096]{0,1:T(8,128)}, ...), branch_computations={%region_153.154_spmd, %region_154.174_spmd} | conditional | flops 4326035456 | bytes 134418288 | solution.py:320
  611.7 41.4 %conditional.11 = (f32[128,1024]{1,0:T(8,128)S(1)}, f32[1024,4096]{0,1:T(8,128)}, f32[4096,1024]{1,0:T(8,128)}, f32[2,1024]{1,0:T(2,128)}, f32[4096]{0:T(1024)}) conditional(s32[]{:T(128)} %convert_element_type.846, (bf16[128,1024]{1,0:T(8,128)(2,1)S(1)}, bf16[4096,1024]{1,0:T(8,128)(2,1)}, f32[4,128,4096]{2,1,0:T(8,128)}, s32[]{:T(128)}, ...), branch_computations={%region_161.162_spmd, %region_163.166_spmd} | conditional | flops 4319608832 | bytes 126157384 | solution.py:270
  611.9 7.8 convert_reduce_fusion.23
  622.6 14.3 %bitcast_add_fusion.3 = f32[1024,4096]{0,1:T(8,128)} fusion(f32[1024,4096]{0,1:T(8,128)} %get-tuple-element.2629, bf16[128,4096]{1,0:T(8,128)(2,1)S(1)} %get-tuple-element.3062, bf16[128,1024]{1,0:T(8,128)(2,1)S(1)} %get-tuple-element.2630), kind=kOutput, calls=%fused_computation.788 | convolution fusion | flops 1077936128 | bytes 34865152 | tf_op jit(solution)/shard_map/cond/branch_1_fun/cond/branch_0_fun/dot_general | solution.py:39
  636.9 14.5 %convolution_add_fusion.11 = f32[4096,1024]{1,0:T(8,128)} fusion(f32[4096,1024]{1,0:T(8,128)} %get-tuple-element.2631, bf16[128,1024]{1,0:T(8,128)(2,1)S(1)} %get-tuple-element.2624, f32[4,128,4096]{2,1,0:T(8,128)} %get-tuple-element.2626, s32[]{:T(128)} %get-tuple-element.2627), kind=kOutput, calls=%fused_computation.789 | convolution fusion | flops 1082654720 | bytes 35914240 | tf_op jit(solution)/shard_map/cond/branch_1_fun/cond/branch_0_fun/dot_general | solution.py:39
  662.6 8.8 collective-permute-start.11
  671.4 12.8 %collective-permute-done.11 = bf16[128,1024]{1,0:T(8,128)(2,1)S(1)} collective-permute-done((bf16[128,1024]{1,0:T(8,128)(2,1)}, bf16[128,1024]{1,0:T(8,128)(2,1)S(1)}, u32[]{:S(2)}, u32[]{:S(2)}) %collective-permute-start.11) | collective-permute-done | bytes 262176 | tf_op jit(solution)/shard_map/ppermute | solution.py:21
  685.1 53.8 %conditional.40 = (f32[128,1024]{1,0:T(8,128)}, f32[1024,4096]{0,1:T(8,128)}, f32[4096,1024]{1,0:T(8,128)}, f32[2,1024]{1,0:T(2,128)}, f32[4096]{0:T(1024)}, /*i...) conditional(s32[]{:T(128)} %convert_element_type.951, (f32[1024,4096]{0,1:T(8,128)}, ...), branch_computations={%region_174.175_spmd, %region_175.195_spmd} | conditional | flops 4326035456 | bytes 134418288 | solution.py:320
  690.0 41.0 %conditional.12 = (f32[128,1024]{1,0:T(8,128)S(1)}, f32[1024,4096]{0,1:T(8,128)}, f32[4096,1024]{1,0:T(8,128)}, f32[2,1024]{1,0:T(2,128)}, f32[4096]{0:T(1024)}) conditional(s32[]{:T(128)} %convert_element_type.863, (bf16[128,1024]{1,0:T(8,128)(2,1)S(1)}, bf16[4096,1024]{1,0:T(8,128)(2,1)}, f32[4,128,4096]{2,1,0:T(8,128)}, s32[]{:T(128)}, ...), branch_computations={%region_182.183_spmd, %region_184.187_spmd} | conditional | flops 4319608832 | bytes 126157384 | solution.py:270
  690.0 7.8 convert_reduce_fusion.27
  700.7 14.3 %bitcast_add_fusion.4 = f32[1024,4096]{0,1:T(8,128)} fusion(f32[1024,4096]{0,1:T(8,128)} %get-tuple-element.2682, bf16[128,4096]{1,0:T(8,128)(2,1)S(1)} %get-tuple-element.3067, bf16[128,1024]{1,0:T(8,128)(2,1)S(1)} %get-tuple-element.2683), kind=kOutput, calls=%fused_computation.897 | convolution fusion | flops 1077936128 | bytes 34865152 | tf_op jit(solution)/shard_map/cond/branch_1_fun/cond/branch_0_fun/dot_general | solution.py:39
  715.0 14.5 %convolution_add_fusion.12 = f32[4096,1024]{1,0:T(8,128)} fusion(f32[4096,1024]{1,0:T(8,128)} %get-tuple-element.2684, bf16[128,1024]{1,0:T(8,128)(2,1)S(1)} %get-tuple-element.2677, f32[4,128,4096]{2,1,0:T(8,128)} %get-tuple-element.2679, s32[]{:T(128)} %get-tuple-element.2680), kind=kOutput, calls=%fused_computation.898 | convolution fusion | flops 1082654720 | bytes 35914240 | tf_op jit(solution)/shard_map/cond/branch_1_fun/cond/branch_0_fun/dot_general | solution.py:39
  742.6 5.4 collective-permute-done.12
  748.9 6.6 conditional.41
  755.5 13.8 %copy.302 = bf16[1024,4096]{1,0:T(8,128)(2,1)} copy(f32[1024,4096]{0,1:T(8,128)} %get-tuple-element.2957) | data formatting | bytes 25165824 | tf_op jit(solution)/shard_map/cond | solution.py:320
  769.3 9.1 convert_element_type.959
  778.5 230.7 %all-reduce.5.cloned.1.call-done = (bf16[1,1024,4096]{2,1,0:T(8,128)(2,1)}, bf16[4096,1024]{1,0:T(8,128)(2,1)}) async-done(((bf16[1,1024,4096]{2,1,0:T(8,128)(2,1)}, bf16[4096,1024]{1,0:T(8,128)(2,1)}), (bf16[1,1024,4096]{2,1,0:T(8,128)(2,1)}, bf16[4096,1024]{1,0:T(8,128)(2,1)})) %all-reduce.5.cloned.1.call-update) | async-done | bytes 16777232 | tf_op jit(solution)/shard_map/psum | solution.py:338
  1009.2 4.6 slice.977
  1018.5 123.6 %all-reduce.1 = (bf16[1,1024]{1,0:T(2,128)(2,1)S(1)}, bf16[1,2,1024]{2,1,0:T(2,128)(2,1)S(1)}, bf16[1,2,1024]{2,1,0:T(2,128)(2,1)S(1)}) all-reduce(bf16[1,1024]{1,0:T(2,128)(2,1)S(1)} %broadcast_in_dim.467, bf16[1,2,1024]{2,1,0:T(2,128)(2,1)S(1)} %convert_bitcast_fusion.9, ...), channel_id=1, replica_groups=mesh['section'=4,'dp'=32] {'dp'}, use_global_device_ids=true, to_apply=%region_221.222 | all-reduce | flops 5120 | bytes 20480 | tf_op jit(solution)/shard_map/psum | solution.py:340
  1145.4 70.1 %all-reduce = (f32[2,2,1024]{2,1,0:T(2,128)}, f32[2,4096]{1,0:T(2,128)}) all-reduce(f32[2,2,1024]{2,1,0:T(2,128)S(1)} %broadcast_multiply_fusion.56, f32[2,4096]{1,0:T(2,128)S(1)} %broadcast_multiply_fusion.55), channel_id=1, replica_groups=mesh['section'=4,'dp'=32] {'section','dp'}, use_global_device_ids=true, to_apply=%region_219.220 | all-reduce | flops 12288 | bytes 98304 | tf_op jit(solution)/shard_map/psum | solution.py:335
  1215.5 11.8 broadcast_in_dim.466
  1227.3 8.8 convert_select_fusion
  (348 shorter events, 223.8 us)
Async XLA Ops:
  8.0 9.7 copy-start
  8.0 7.9 copy-start.87
  8.0 1001.2 %all-reduce.5.cloned.1.call-start = ((), (), s32[]{:S(2)}) async-start(), calls=%async_computation.2 | async-start | bytes 33554432 | tf_op jit(solution)/shard_map/psum | solution.py:338
  8.1 93.8 %collective-permute-start = (bf16[2048,1024]{1,0:T(8,128)(2,1)}, bf16[2048,1024]{1,0:T(8,128)(2,1)}, u32[]{:S(2)}, u32[]{:S(2)}) collective-permute-start(bf16[2048,1024]{1,0:T(8,128)(2,1)} %param.106), channel_id=1, source_target_pairs={{0,32},{32,64},{64,96},{1,33},{33,65},{65,97},{2,34},{34,66},{66,9... | collective-permute-start | bytes 12582920 | tf_op jit(solution)/shard_map/ppermute | solution.py:21
  17.7 88.8 %copy-start.32 = (bf16[2048,1024]{1,0:T(8,128)(2,1)S(1)}, bf16[2048,1024]{1,0:T(8,128)(2,1)}, u32[]{:S(2)}) copy-start(bf16[2048,1024]{1,0:T(8,128)(2,1)} %param.106) | copy-start | bytes 12582916
  106.5 2.5 copy-start.68
  106.5 2.5 copy-start.95
  106.5 2.5 copy-start.97
  112.9 16.5 %collective-permute-start.1 = (bf16[128,1024]{1,0:T(8,128)(2,1)S(1)}, bf16[128,1024]{1,0:T(8,128)(2,1)S(1)}, u32[]{:S(2)}, u32[]{:S(2)}) collective-permute-start(bf16[128,1024]{1,0:T(8,128)(2,1)S(1)} %convert_element_type.927), channel_id=1, source_target_pairs={{0,32},{32,64},{64,96},{1,33},{33,65},{65,97},{2,34},{34,66},{66,9... | collective-permute-start | bytes 786440 | tf_op jit(solution)/shard_map/ppermute | solution.py:21
  117.7 13.5 %copy-start.9 = (f32[4,128,4096]{2,1,0:T(8,128)}, f32[4,128,4096]{2,1,0:T(8,128)S(1)}, u32[]{:S(2)}) copy-start(f32[4,128,4096]{2,1,0:T(8,128)S(1)} %bitcast_dynamic-update-slice_fusion.6) | copy-start | bytes 25165828
  119.6 9.8 copy-start.93
  120.8 10.4 copy-start.10
  148.6 4.3 copy-start.11
  148.7 17.6 %collective-permute-start.2 = (bf16[128,1024]{1,0:T(8,128)(2,1)S(1)}, bf16[128,1024]{1,0:T(8,128)(2,1)S(1)}, u32[]{:S(2)}, u32[]{:S(2)}) collective-permute-start(bf16[128,1024]{1,0:T(8,128)(2,1)S(1)} %convert_element_type.929), channel_id=1, source_target_pairs={{0,32},{32,64},{64,96},{1,33},{33,65},{65,97},{2,34},{34,66},{66,9... | collective-permute-start | bytes 786440 | tf_op jit(solution)/shard_map/ppermute | solution.py:21
  156.1 3.2 copy-start.94
  184.3 4.3 copy-start.12
  184.4 20.9 %collective-permute-start.3 = (bf16[128,1024]{1,0:T(8,128)(2,1)S(1)}, bf16[128,1024]{1,0:T(8,128)(2,1)S(1)}, u32[]{:S(2)}, u32[]{:S(2)}) collective-permute-start(bf16[128,1024]{1,0:T(8,128)(2,1)S(1)} %convert_element_type.931), channel_id=1, source_target_pairs={{0,32},{32,64},{64,96},{1,33},{33,65},{65,97},{2,34},{34,66},{66,9... | collective-permute-start | bytes 786440 | tf_op jit(solution)/shard_map/ppermute | solution.py:21
  191.8 3.2 copy-start.83
  235.7 4.3 copy-start.13
  235.7 20.9 %collective-permute-start.4 = (bf16[128,1024]{1,0:T(8,128)(2,1)S(1)}, bf16[128,1024]{1,0:T(8,128)(2,1)S(1)}, u32[]{:S(2)}, u32[]{:S(2)}) collective-permute-start(bf16[128,1024]{1,0:T(8,128)(2,1)S(1)} %convert_element_type.933), channel_id=1, source_target_pairs={{0,32},{32,64},{64,96},{1,33},{33,65},{65,97},{2,34},{34,66},{66,9... | collective-permute-start | bytes 786440 | tf_op jit(solution)/shard_map/ppermute | solution.py:21
  243.1 3.2 copy-start.84
  274.7 4.3 copy-start.14
  274.7 14.7 %collective-permute-start.5 = (bf16[128,1024]{1,0:T(8,128)(2,1)S(1)}, bf16[128,1024]{1,0:T(8,128)(2,1)S(1)}, u32[]{:S(2)}, u32[]{:S(2)}) collective-permute-start(bf16[128,1024]{1,0:T(8,128)(2,1)S(1)} %convert_element_type.935), channel_id=1, source_target_pairs={{0,32},{32,64},{64,96},{1,33},{33,65},{65,97},{2,34},{34,66},{66,9... | collective-permute-start | bytes 786440 | tf_op jit(solution)/shard_map/ppermute | solution.py:21
  282.1 3.2 copy-start.85
  294.7 22.4 %copy-start.15 = (f32[1,128,4096]{2,1,0:T(8,128)S(1)}, f32[1,128,4096]{2,1,0:T(8,128)}, u32[]{:S(2)}) copy-start(f32[1,128,4096]{2,1,0:T(8,128)} %constant_dynamic-slice_fusion.13) | copy-start | bytes 6291460
  294.8 29.6 %collective-permute-start.6 = (bf16[128,1024]{1,0:T(8,128)(2,1)S(1)}, bf16[128,1024]{1,0:T(8,128)(2,1)S(1)}, u32[]{:S(2)}, u32[]{:S(2)}) collective-permute-start(bf16[128,1024]{1,0:T(8,128)(2,1)S(1)} %convert_element_type.937), channel_id=1, source_target_pairs={{0,32},{32,64},{64,96},{1,33},{33,65},{65,97},{2,34},{34,66},{66,9... | collective-permute-start | bytes 786440 | tf_op jit(solution)/shard_map/ppermute | solution.py:21
  318.7 3.2 copy-start.86
  329.2 3.0 copy-start.16
  359.9 0.8 copy-start.18
  361.4 9.2 collective-permute-start.7
  382.1 81.9 %collective-permute-start.8 = (bf16[128,1024]{1,0:T(8,128)(2,1)}, bf16[128,1024]{1,0:T(8,128)(2,1)S(1)}, u32[]{:S(2)}, u32[]{:S(2)}) collective-permute-start(bf16[128,1024]{1,0:T(8,128)(2,1)} %convert_element_type.943), channel_id=1, source_target_pairs={{32,0},{64,32},{96,64},{33,1},{65,33},{97,65},{34,2},{66,34},{98,6... | collective-permute-start | bytes 786440 | tf_op jit(solution)/shard_map/ppermute | solution.py:21
  469.7 7.8 copy-start.4
  520.4 14.8 %collective-permute-start.9 = (bf16[128,1024]{1,0:T(8,128)(2,1)}, bf16[128,1024]{1,0:T(8,128)(2,1)S(1)}, u32[]{:S(2)}, u32[]{:S(2)}) collective-permute-start(bf16[128,1024]{1,0:T(8,128)(2,1)} %convert_element_type.946), channel_id=1, source_target_pairs={{32,0},{64,32},{96,64},{33,1},{65,33},{97,65},{34,2},{66,34},{98,6... | collective-permute-start | bytes 786440 | tf_op jit(solution)/shard_map/ppermute | solution.py:21
  540.9 7.8 copy-start.5
  586.4 19.6 %collective-permute-start.10 = (bf16[128,1024]{1,0:T(8,128)(2,1)}, bf16[128,1024]{1,0:T(8,128)(2,1)S(1)}, u32[]{:S(2)}, u32[]{:S(2)}) collective-permute-start(bf16[128,1024]{1,0:T(8,128)(2,1)} %convert_element_type.949), channel_id=1, source_target_pairs={{32,0},{64,32},{96,64},{33,1},{65,33},{97,65},{34,2},{66,34},{98,6... | collective-permute-start | bytes 786440 | tf_op jit(solution)/shard_map/ppermute | solution.py:21
  611.9 7.8 copy-start.6
  662.6 21.6 %collective-permute-start.11 = (bf16[128,1024]{1,0:T(8,128)(2,1)}, bf16[128,1024]{1,0:T(8,128)(2,1)S(1)}, u32[]{:S(2)}, u32[]{:S(2)}) collective-permute-start(bf16[128,1024]{1,0:T(8,128)(2,1)} %convert_element_type.952), channel_id=1, source_target_pairs={{32,0},{64,32},{96,64},{33,1},{65,33},{97,65},{34,2},{66,34},{98,6... | collective-permute-start | bytes 786440 | tf_op jit(solution)/shard_map/ppermute | solution.py:21
  690.0 7.8 copy-start.7
  740.7 7.3 collective-permute-start.12
  778.4 457.8 %reduce-scatter.2.cloned.1.call-start = ((), (), s32[]{:S(2)}) async-start(), calls=%async_computation.1 | async-start | bytes 1310720 | tf_op jit(solution)/shard_map/reduce_scatter | solution.py:326
  1013.8 2.5 copy-start.19
  1013.8 213.5 %collective-permute-start.13 = (bf16[2048,1024]{1,0:T(8,128)(2,1)}, bf16[2048,1024]{1,0:T(8,128)(2,1)}, u32[]{:S(2)}, u32[]{:S(2)}) collective-permute-start(bf16[2048,1024]{1,0:T(8,128)(2,1)} %slice.977), channel_id=1, source_target_pairs={{32,0},{64,32},{96,64},{33,1},{65,33},{97,65},{34,2},{66,34},{98,6... | collective-permute-start | bytes 12582920 | tf_op jit(solution)/shard_map/ppermute | solution.py:21
  1227.3 8.9 copy-start.1
Sparse Core Ops, SparseCore 0:
  778.5 230.6 all-reduce.4
Sparse Core Ops, SparseCore 1:
  1018.5 31.2 reduce-scatter.1
where the time goes:
time: 1250 us; the launch traced here: 1240 us
  waiting for transfers between devices  470 us (38%)
  matrix products  204 us (16%)
  blocking collectives  194 us (16%)
  other arithmetic  147 us (12%)
  local copies, waits for them, and re-layouts  98.9 us (8%)
  starting transfers between devices  61.2 us (5%)
  loops' own time  51.9 us (4%)
  between operations  17.3 us (1%)
    ppermute x14, waiting for transfers between devices, passed_along(): lax.ppermute(value, axis, [(source, source + steps) for source in range(i...  239 us
    psum x1, waiting for transfers between devices, on_device(): lax.psum(first_sum.astype(jnp.bfloat16), 'dp').astype(jnp.float32)  231 us
    psum x1, blocking collectives, on_device(): lax.psum(branch_sum.astype(jnp.bfloat16), 'dp').astype(jnp.float32)  124 us
    dot_general x8, matrix products, contract_rows(): lax.dot_general(left_side, right_side, (((0,), (0,)), ((), ())), preferre...  115 us
    psum x1, blocking collectives, on_device(): lax.psum((pair_full, hidden_full), ('section', 'dp'))  70.1 us
    ppermute x14, starting transfers between devices, passed_along(): lax.ppermute(value, axis, [(source, source + steps) for source in range(i...  61.1 us
    dynamic_update_slice x41, other arithmetic, place_slot(): lax.dynamic_update_index_in_dim(buffer, jnp.where(running, entries, previ...  43.8 us
    dot_general x8, matrix products, contract_columns(): lax.dot_general(left_side, right_side, (((1,), (1,)), ((), ())), preferre...  42.6 us
  transfers between devices with their start and end apart: 16, of which 12 were waited for; matrix products, arithmetic and copies ran while one was open for 8% of the time, Pallas kernels for 0%

commit v1 on v0

v1 whole, which is shorter than its diff:
```python
import math

import jax
import jax.numpy as jnp
from jax import lax
from jax.experimental import pallas as pl
from jax.experimental.pallas import tpu as pltpu
from jax.sharding import PartitionSpec as P

MESH = pl.DeviceIdType.MESH
BF16 = jnp.bfloat16
F32 = jnp.float32

WIDTH = 1024
FF = 4096
LEN = 128
SLOTS = 4
ROWS = SLOTS * LEN
PAIRS = 8
SECTIONS = 4
NORM_EPS = 1e-05
GELU_C = math.sqrt(2.0 / math.pi)
CHUNKS = 8
ORDER = (10, 0, 8, 3, 4, 5, 1, 9, 6, 7, 2)
OFFSET = (0, 1, 2, 4, 5, 6, 7, 8, 11, 13, 20)


def device(section, x, y, core):
    return (section, x * 8 + y * 2 + core)


def place():
    at = lax.axis_index("dp")
    return lax.axis_index("section"), at // 8, (at // 2) % 4, at % 2


def neighbours(section, x, y, core):
    found = [device(section, x, y, 1 - core)]
    for d in (1, 2, 3):
        found.append(device(section, (x + d) % 4, y, core))
        found.append(device(section, x, (y + d) % 4, core))
        found.append(device((section + d) % 4, x, y, core))
    return found


def greet(section, x, y, core):
    barrier = pltpu.get_barrier_semaphore()
    others = neighbours(section, x, y, core)
    for other in others:
        pl.semaphore_signal(barrier, inc=1, device_id=other, device_id_type=MESH)
    pl.semaphore_wait(barrier, len(others))


def remote(source, target, send_sem, recv_sem, to):
    return pltpu.make_async_remote_copy(
        src_ref=source,
        dst_ref=target,
        send_sem=send_sem,
        recv_sem=recv_sem,
        device_id=to,
        device_id_type=MESH,
    )


def dot(a, b):
    return jnp.dot(a, b, preferred_element_type=F32)


def dot_nt(a, b):
    return lax.dot_general(a, b, (((1,), (1,)), ((), ())), preferred_element_type=F32)


def dot_tn(a, b):
    return lax.dot_general(a, b, (((0,), (0,)), ((), ())), preferred_element_type=F32)


def normalize(entries):
    average = jnp.mean(entries, axis=-1, keepdims=True)
    centered = entries - average
    inverse = lax.rsqrt(jnp.mean(centered * centered, axis=-1, keepdims=True) + NORM_EPS)
    return centered * inverse, inverse


def norm_backward(grad_out, unit, inverse, gain):
    scaled = grad_out * gain
    middle = jnp.mean(scaled, axis=-1, keepdims=True)
    along = jnp.mean(scaled * unit, axis=-1, keepdims=True)
    return inverse * (scaled - middle - unit * along)


def column_sum(entries):
    return jnp.sum(entries, axis=0, keepdims=True)


def mega_kernel(
    block_hbm, cot_hbm, group_hbm, live_hbm, scale_hbm, gains_hbm, shifts_hbm, qv_hbm, up_hbm, bias_hbm, w1_hbm, down_hbm,
    out_hbm, small_hbm, grad_hbm,
    group_ids, live_count, group_scale, gains, shifts, qv_bias, up_bias, out_bias,
    w1, buffer, w2t, ops, units, inverses, r_in, r_out, g_in, g_out, wide, small, vectors,
    pair, r1, r2, r3, r4, z, sx, sy, ss, sums,
    load_sem, down_send, down_recv, ag_send, ag_recv,
    fwd_send, fwd_recv, bwd_send, bwd_recv, ig_send, ig_recv,
    pair_send, pair_recv, pair_free, ring_send, ring_recv, z_send, z_recv, own_sem, last_send, last_recv,
    tiny_send, tiny_recv,
):
    section, x, y, core = place()
    parity = section % 2
    layer = section // 2
    last = section == SECTIONS - 1
    first = section == 0
    sibling = device(section, x, y, 1 - core)
    w1t, w2 = buffer.at[pl.ds(0, FF)], buffer.at[pl.ds(FF, FF)]

    load_w1 = pltpu.make_async_copy(w1_hbm.at[0], w1, load_sem.at[0])
    load_own = pltpu.make_async_copy(down_hbm, w2.at[pl.ds(2048, 2048)], load_sem.at[1])
    load_block = pltpu.make_async_copy(block_hbm, r_in, load_sem.at[2])
    load_cot = pltpu.make_async_copy(cot_hbm, g_in, load_sem.at[3])

    pieces = [
        (gains_hbm, gains), (shifts_hbm, shifts), (bias_hbm, out_bias), (qv_hbm, qv_bias), (up_hbm, up_bias),
        (group_hbm, group_ids), (live_hbm, live_count), (scale_hbm, group_scale),
    ]
    load_pieces = [pltpu.make_async_copy(*piece, load_sem.at[4 + j]) for j, piece in enumerate(pieces)]

    @pl.when(first)
    def _():
        load_block.start()

    for copy in load_pieces:
        copy.start()
    load_w1.start()

    @pl.when(parity == 1)
    def _():
        load_own.start()

    @pl.when(last)
    def _():
        load_cot.start()

    greet(section, x, y, core)

    row_a = core * 512 + y * 128 + x * 32
    row_b = 1024 + core * 512 + x * 128 + y * 32

    def down_copy(half):
        row = row_a if half == 0 else row_b
        return remote(
            down_hbm.at[pl.ds(row, 32)], w2.at[pl.ds(row, 32)], down_send.at[half], down_recv.at[half],
            device((section + 1) % 4, x, y, core),
        )

    def ag_copy(index):
        d = index % 3 + 1
        along_x = device(section, (x + d) % 4, y, core)
        along_y = device(section, x, (y + d) % 4, core)
        if index < 3:
            rows, to = pl.ds(row_a, 32), along_x
        elif index < 6:
            rows, to = pl.ds(row_b, 32), along_y
        elif index < 9:
            rows, to = pl.ds(core * 512 + y * 128, 128), along_y
        elif index < 12:
            rows, to = pl.ds(1024 + core * 512 + x * 128, 128), along_x
        elif index < 16:
            rows, to = pl.ds(core * 512 + (y + index - 12) % 4 * 128, 128), sibling
        else:
            rows, to = pl.ds(1024 + core * 512 + (x + index - 16) % 4 * 128, 128), sibling
        return remote(w2.at[rows], w2.at[rows], ag_send.at[index], ag_recv.at[index], to)

    @pl.when(parity == 0)
    def _():
        down_copy(0).start()
        down_copy(1).start()

    for copy in load_pieces:
        copy.wait()

    @pl.when(parity == 0)
    def _():
        vectors[5:6, :] = qv_bias[layer, 0:1, :]
        vectors[6:7, :] = jnp.zeros((1, WIDTH), F32)
        vectors[7:8, :] = qv_bias[layer, 1:2, :]

    @pl.when(parity == 1)
    def _():
        for j in range(4):
            vectors[5 + j : 6 + j, :] = up_bias[pl.ds(layer, 1), j * WIDTH : (j + 1) * WIDTH]

    def sequence_weight(micro):
        group = group_ids[micro]
        chosen = jnp.float32(0.0)
        for label in range(8):
            chosen = jnp.where(group == label, group_scale[label], chosen)
        weight = jnp.where(micro < live_count[0], chosen, 0.0)
        return jnp.where(last, weight, 1.0)

    small[...] = jnp.zeros_like(small)

    def gather_start():
        for half in (0, 1):
            down_copy(half).wait_recv()
            for index in range(3 * half, 3 * half + 3):
                ag_copy(index).start()
        for half in (0, 1):
            for index in range(3 * half, 3 * half + 3):
                ag_copy(index).wait()
            for index in range(6 + 3 * half, 9 + 3 * half):
                ag_copy(index).start()
            ag_copy(12 + 4 * half).start()
        load_own.wait()

    def gather_end():
        for d in (1, 3, 2):
            for half in (0, 1):
                ag_copy(5 + 3 * half + 4 - d).wait()
                ag_copy(12 + 4 * half + d).start()
        for index in range(12, 20):
            ag_copy(index).wait()

    pl.when(parity == 1)(gather_start)
    pl.when(last)(gather_end)

    @pl.when(parity == 0)
    def _():
        down_copy(0).wait_send()
        down_copy(1).wait_send()

    load_w1.wait()

    @pl.when(first)
    def _():
        load_block.wait()

    @pl.when(last)
    def _():
        load_cot.wait()

    def fwd_copy(micro):
        return remote(
            r_out.at[micro], r_in.at[micro], fwd_send.at[micro], fwd_recv.at[micro],
            device((section + 1) % 4, x, y, core),
        )

    def bwd_copy(micro):
        return remote(
            g_out.at[micro], g_in.at[micro], bwd_send.at[micro], bwd_recv.at[micro],
            device((section + 3) % 4, x, y, core),
        )

    def ig_copy(micro, d):
        to = (section + d) % 4
        return remote(
            g_out.at[micro, :, pl.ds(d * 256, 256)], grad_hbm.at[micro], ig_send.at[micro, d], ig_recv.at[micro],
            device(to, x, y, core),
        )

    def ig_own(micro):
        return pltpu.make_async_copy(g_out.at[micro, :, pl.ds(0, 256)], grad_hbm.at[micro], ig_send.at[micro, 0])

    lanes = lax.broadcasted_iota(jnp.int32, (LEN, 128), 1)
    low_lanes = lanes < 64

    def two_heads(entries):
        zero = jnp.zeros_like(entries)
        return jnp.concatenate([jnp.where(low_lanes, entries, zero), jnp.where(low_lanes, zero, entries)], axis=0)

    def transposes():
        def one(j, carry):
            cut = pl.ds(pl.multiple_of(j * 256, 256), 256)
            w1t[cut, :] = w1[:, cut].T
            return carry

        lax.fori_loop(0, 16, one, 0)

        @pl.when(parity == 1)
        def _():
            def two(j, carry):
                cut = pl.ds(pl.multiple_of(j * 256, 256), 256)
                w2t[:, cut] = w2[cut, :].T
                return carry

            lax.fori_loop(0, 16, two, 0)

    def attention_forward(micro):
        normed = ops[0, micro]
        for j in range(3):
            part = dot(normed, w1[:, j * WIDTH : (j + 1) * WIDTH]) + vectors[5 + j : 6 + j, :]
            ops[6 + j, micro] = part.astype(BF16)
        rows = lax.broadcasted_iota(jnp.int32, (LEN, 256), 0)
        columns = lax.broadcasted_iota(jnp.int32, (LEN, 256), 1) % 128
        causal = rows >= columns
        for p in range(PAIRS):
            cut = slice(p * 128, (p + 1) * 128)
            query, key, value = (ops[6 + j, micro, :, cut] for j in range(3))
            scores = dot_nt(query, two_heads(key)) * 0.125
            scores = jnp.where(causal, scores, -1e9)
            halves = []
            for half in (scores[:, :128], scores[:, 128:]):
                powers = jnp.exp(half - jnp.max(half, axis=-1, keepdims=True))
                halves.append((powers / jnp.sum(powers, axis=-1, keepdims=True)).astype(BF16))
            weights = jnp.concatenate(halves, axis=1)
            ops[3 + p // 4, micro, :, (p % 4) * 256 : (p % 4 + 1) * 256] = weights
            ops[2, micro, :, cut] = dot(weights, two_heads(value)).astype(BF16)
        wide[...] = dot_nt(ops[2, micro], w1[:, 3 * WIDTH :]) + out_bias[...]

    def feed_forward(micro):
        normed = ops[0, micro]
        branch = out_bias[...]
        for j in (2, 3, 0, 1):
            hidden = dot(normed, w1[:, j * WIDTH : (j + 1) * WIDTH]) + vectors[5 + j : 6 + j, :]
            square = hidden * hidden
            along = jnp.tanh(hidden * (GELU_C + (GELU_C * 0.044715) * square))
            above = 0.5 * (1.0 + along)
            slope = above + 0.5 * hidden * (1.0 - along * along) * (GELU_C + (3.0 * GELU_C * 0.044715) * square)
            active = (hidden * above).astype(BF16)
            ops[6 + j, micro] = slope.astype(BF16)
            ops[2 + j, micro] = active
        for j in (2, 3, 0, 1):
            if j == 0:
                pl.when((micro == 0) & (section == 1))(gather_end)
            branch = branch + dot(ops[2 + j, micro], w2[j * WIDTH : (j + 1) * WIDTH, :])
        wide[...] = branch

    def attention_backward(micro):
        ops[9, micro] = dot(ops[1, micro], w1[:, 3 * WIDTH :]).astype(BF16)
        for p in range(PAIRS):
            cut = slice(p * 128, (p + 1) * 128)
            query, key, value = (ops[6 + j, micro, :, cut] for j in range(3))
            grad = ops[9, micro, :, cut]
            weights = ops[3 + p // 4, micro, :, (p % 4) * 256 : (p % 4 + 1) * 256]
            grad_weights = dot_nt(grad, two_heads(value))
            weights_wide = weights.astype(F32)
            product = weights_wide * grad_weights
            left = product[:, :128] - weights_wide[:, :128] * jnp.sum(product[:, :128], axis=-1, keepdims=True)
            right = product[:, 128:] - weights_wide[:, 128:] * jnp.sum(product[:, 128:], axis=-1, keepdims=True)
            grad_scores = jnp.concatenate([left, right], axis=1).astype(BF16)
            grad_query = dot(grad_scores, two_heads(key)) * 0.125
            both = dot_tn(grad_scores, query) * 0.125
            grad_key = jnp.where(low_lanes, both[:128], both[128:])
            both = dot_tn(weights, grad)
            grad_value = jnp.where(low_lanes, both[:128], both[128:])
            for j, part in enumerate((grad_query, grad_key, grad_value)):
                ops[6 + j, micro, :, cut] = part.astype(BF16)
        total = jnp.zeros((LEN, WIDTH), F32)
        for j in range(3):
            part = ops[6 + j, micro]
            total = total + dot(part, w1t[j * WIDTH : (j + 1) * WIDTH, :])
            if j != 1:
                small[5 + j : 6 + j, :] += column_sum(part.astype(F32))
        wide[...] = total

    def feed_backward(micro):
        grad_branch = ops[1, micro]
        total = jnp.zeros((LEN, WIDTH), F32)
        for j in range(4):
            grad = dot(grad_branch, w2t[:, j * WIDTH : (j + 1) * WIDTH])
            grad = (grad * ops[6 + j, micro].astype(F32)).astype(BF16)
            ops[6 + j, micro] = grad
            small[5 + j : 6 + j, :] += column_sum(grad.astype(F32))
            total = total + dot(grad, w1t[j * WIDTH : (j + 1) * WIDTH, :])
        wide[...] = total

    def forward(micro):
        @pl.when(jnp.logical_not(first))
        def _():
            fwd_copy(micro).wait_recv()

        residual = r_in[micro].astype(F32)
        unit, _ = normalize(residual)
        ops[0, micro] = (unit * gains[0, 0:1, :] + shifts[0, 0:1, :]).astype(BF16)

        @pl.when(parity == 0)
        def _():
            attention_forward(micro)

        @pl.when(parity == 1)
        def _():
            feed_forward(micro)

        unit, inverse = normalize(wide[...])
        units[micro] = unit.astype(BF16)
        inverses[micro] = inverse

        @pl.when(jnp.logical_not(last))
        def _():
            r_out[micro] = (r_in[micro].astype(F32) + unit * gains[0, 1:2, :] + shifts[0, 1:2, :]).astype(BF16)
            fwd_copy(micro).start()

    def backward(micro):
        @pl.when(jnp.logical_not(last))
        def _():
            bwd_copy(micro).wait_recv()

        incoming = g_in[micro].astype(F32) * sequence_weight(micro)
        unit = units[micro].astype(F32)
        small[1:2, :] += column_sum(incoming * unit)
        small[3:4, :] += column_sum(incoming)
        grad_branch = norm_backward(incoming, unit, inverses[micro], gains[0, 1:2, :]).astype(BF16)
        ops[1, micro] = grad_branch
        small[4:5, :] += column_sum(grad_branch.astype(F32))

        @pl.when(parity == 0)
        def _():
            attention_backward(micro)

        @pl.when(parity == 1)
        def _():
            feed_backward(micro)

        grad_normed = wide[...]
        unit, inverse = normalize(r_in[micro].astype(F32))
        small[0:1, :] += column_sum(grad_normed * unit)
        small[2:3, :] += column_sum(grad_normed)
        incoming = g_in[micro].astype(F32) * sequence_weight(micro)
        grad = incoming + norm_backward(grad_normed, unit, inverse, gains[0, 0:1, :])
        g_out[micro] = grad.astype(BF16)

        @pl.when(jnp.logical_not(first))
        def _():
            bwd_copy(micro).start()

        @pl.when(first)
        def _():
            ig_own(micro).start()
            for d in (1, 2, 3):
                ig_copy(micro, d).start()

    turn_at = jnp.where(section >= 2, 0, SLOTS)

    def step(t, carry):
        is_forward = jnp.where(last, (t + 1) % 2, jnp.where(t < SLOTS, 1, 0))
        micro = jnp.where(last, t // 2, t % SLOTS)

        @pl.when(t == turn_at)
        def _():
            transposes()

        @pl.when(is_forward == 1)
        def _():
            forward(micro)

        @pl.when(is_forward == 0)
        def _():
            backward(micro)

        return carry

    lax.fori_loop(0, 2 * SLOTS, step, 0)

    def spot(h):
        return (x, y) if h == 0 else (y, x)

    def peer(axis, d):
        if axis == 0:
            return device(section, (x + d) % 4, y, core)
        return device(section, x, (y + d) % 4, core)

    def at(k, h, b1, b2, n, c=None):
        c = core if c is None else c
        row = k * 1024 + c * 512 + h * 256 + b1 * 64 + b2 * 16
        return pl.ds(pl.multiple_of(row, 16), n)

    def out_chunk(k):
        return jnp.where(parity == 1, k - 2, jnp.where(k < 2, k, k - 2))

    left, right = pl.ds(0, 512), pl.ds(512, 512)

    def ring(stage, k, h, d, source, target, to):
        return remote(source, target, ring_send.at[stage, k, h, d], ring_recv.at[stage, k, h, d], to)

    def pair_copy(k):
        rows = at(k, 0, 0, 0, 512, 1 - core)
        return remote(buffer.at[rows], pair.at[k % 2], pair_send.at[k], pair_recv.at[k], sibling)

    def rs_one(k, h, d):
        p1, _ = spot(h)
        rows = at(k, h, (p1 + 2) % 4, 0, 64)
        return ring(0, k, h, d, buffer.at[rows, left if d == 0 else right], r1.at[k, h, d], peer(h, 1 - 2 * d))

    def rs_two(k, h, d):
        p1, _ = spot(h)
        step = 1 - 2 * d
        return ring(1, k, h, d, buffer.at[at(k, h, (p1 + step) % 4, 0, 64)], r2.at[k, h, d], peer(h, step))

    def rs_three(k, h, d):
        p1, p2 = spot(h)
        rows = at(k, h, p1, (p2 + 2) % 4, 16)
        return ring(2, k, h, d, buffer.at[rows, left if d == 0 else right], r3.at[k, h, d], peer(1 - h, 1 - 2 * d))

    def rs_four(k, h, d):
        p1, p2 = spot(h)
        step = 1 - 2 * d
        return ring(3, k, h, d, buffer.at[at(k, h, p1, (p2 + step) % 4, 16)], r4.at[k, h, d], peer(1 - h, step))

    def z_copy(k, h):
        p1, p2 = spot(h)
        return remote(
            buffer.at[at(k, h, p1, p2, 16)], z.at[k, h], z_send.at[k, h], z_recv.at[k, h],
            device((section + 3) % 4, x, y, core),
        )

    def own_copy(k, h):
        p1, p2 = spot(h)
        return pltpu.make_async_copy(
            buffer.at[at(k, h, p1, p2, 16)], out_hbm.at[at(out_chunk(k), h, p1, p2, 16)], own_sem.at[k, h]
        )

    def ag_one(k, h, d):
        p1, p2 = spot(h)
        return ring(
            4, k, h, d, buffer.at[at(k, h, p1, p2, 16)], out_hbm.at[at(out_chunk(k), h, p1, p2, 16)], peer(1 - h, 1 - 2 * d)
        )

    def ag_two(k, h, d):
        p1, p2 = spot(h)
        step = 1 - 2 * d
        piece = out_hbm.at[at(out_chunk(k), h, p1, (p2 - step) % 4, 16), left if d == 0 else right]
        return ring(5, k, h, d, piece, piece, peer(1 - h, step))

    def ag_three(k, h, d):
        p1, _ = spot(h)
        piece = out_hbm.at[at(out_chunk(k), h, p1, 0, 64)]
        return ring(6, k, h, d, piece, piece, peer(h, 1 - 2 * d))

    def ag_four(k, h, d):
        p1, _ = spot(h)
        step = 1 - 2 * d
        piece = out_hbm.at[at(out_chunk(k), h, (p1 - step) % 4, 0, 64), left if d == 0 else right]
        return ring(7, k, h, d, piece, piece, peer(h, step))

    def last_copy(k):
        piece = out_hbm.at[at(out_chunk(k), 0, 0, 0, 512)]
        return remote(piece, piece, last_send.at[k], last_recv.at[k], sibling)

    both = [(h, d) for h in (0, 1) for d in (0, 1)]

    def stage_0(k):
        feed_down = (parity == 1) & (k < 4)
        from_context = (parity == 0) & (k == 7)
        a = jnp.where(feed_down, 2 + k, jnp.where(from_context, 1, 0))
        b = jnp.where(feed_down, 1, jnp.where(from_context, 2, 2 + k))
        right_side = ops[b].reshape(ROWS, WIDTH)
        for cut in range(4):
            left_side = ops[a, :, :, cut * 256 : (cut + 1) * 256].reshape(ROWS, 256)
            product = dot_tn(left_side, right_side)
            buffer[pl.ds(pl.multiple_of(k * 1024 + cut * 256, 256), 256), :] = product.astype(BF16)
        pl.when(k >= 6 - 4 * parity)(lambda: pl.semaphore_wait(pair_free, 1))
        pair_copy(k).start()

    def stage_1(k):
        pair_copy(k).wait()
        rows = at(k, 0, 0, 0, 512)
        buffer[rows, :] = buffer[rows, :] + pair[k % 2]

        @pl.when(k < CHUNKS - 2)
        def _():
            pl.semaphore_signal(pair_free, inc=1, device_id=sibling, device_id_type=MESH)

        for h, d in both:
            rs_one(k, h, d).start()

    def stage_2(k):
        for h, d in both:
            rs_one(k, h, d).wait()
            p1, _ = spot(h)
            rows = at(k, h, (p1 + 1 - 2 * d) % 4, 0, 64)
            cut = left if d == 0 else right
            buffer[rows, cut] = buffer[rows, cut] + r1[k, h, d]
            rs_two(k, h, d).start()

    def stage_3(k):
        for h in (0, 1):
            p1, _ = spot(h)
            for d in (0, 1):
                rs_two(k, h, d).wait()
            rows = at(k, h, p1, 0, 64)
            total = buffer[rows, :].astype(F32) + r2[k, h, 0].astype(F32) + r2[k, h, 1].astype(F32)
            buffer[rows, :] = total.astype(BF16)
            for d in (0, 1):
                rs_three(k, h, d).start()

    def stage_4(k):
        for h, d in both:
            rs_three(k, h, d).wait()
            p1, p2 = spot(h)
            rows = at(k, h, p1, (p2 + 1 - 2 * d) % 4, 16)
            cut = left if d == 0 else right
            buffer[rows, cut] = buffer[rows, cut] + r3[k, h, d]
            rs_four(k, h, d).start()

    def spread(k):
        for h in (0, 1):
            own_copy(k, h).start()
            for d in (0, 1):
                ag_one(k, h, d).start()

    def stage_5(k):
        @pl.when((parity == 1) | (k >= 4))
        def _():
            for h in (0, 1):
                p1, p2 = spot(h)
                for d in (0, 1):
                    rs_four(k, h, d).wait()
                rows = at(k, h, p1, p2, 16)
                total = buffer[rows, :].astype(F32) + r4[k, h, 0].astype(F32) + r4[k, h, 1].astype(F32)
                buffer[rows, :] = total.astype(BF16)

        @pl.when((parity == 1) & (k < 2))
        def _():
            for h in (0, 1):
                z_copy(k, h).start()

        @pl.when((parity == 0) & (k < 2))
        def _():
            for h in (0, 1):
                p1, p2 = spot(h)
                z_copy(k, h).wait_recv()
                buffer[at(k, h, p1, p2, 16), :] = z[k, h]

        @pl.when(((parity == 1) & (k >= 2)) | (parity == 0))
        def _():
            spread(k)

    def stage_6(k):
        for h in (0, 1):
            for d in (0, 1):
                ag_one(k, h, d).wait()
            for d in (0, 1):
                ag_two(k, h, d).start()
            own_copy(k, h).wait()

    def stage_7(k):
        for h in (0, 1):
            for d in (0, 1):
                ag_two(k, h, d).wait()
            for d in (0, 1):
                ag_three(k, h, d).start()

    def stage_8(k):
        for h in (0, 1):
            for d in (0, 1):
                ag_three(k, h, d).wait()
            for d in (0, 1):
                ag_four(k, h, d).start()

    def stage_9(k):
        for h, d in both:
            ag_four(k, h, d).wait()
        last_copy(k).start()

    def stage_10(k):
        last_copy(k).wait()

    stages = [stage_0, stage_1, stage_2, stage_3, stage_4, stage_5, stage_6, stage_7, stage_8, stage_9, stage_10]

    def tiny(phase, d):
        if phase == 0:
            return remote(small, sx.at[d - 1], tiny_send.at[d - 1], tiny_recv.at[d - 1], peer(0, d))
        if phase == 1:
            return remote(sums.at[0], sy.at[d - 1], tiny_send.at[d + 2], tiny_recv.at[d + 2], peer(1, d))
        if phase == 2:
            return remote(sums.at[1], ss, tiny_send.at[6], tiny_recv.at[6], sibling)
        return remote(
            sums.at[2], small_hbm.at[section], tiny_send.at[6 + d], tiny_recv.at[6 + d],
            device((section + d) % 4, x, y, core),
        )

    keep_own = [
        pltpu.make_async_copy(sums.at[2], small_hbm.at[section], tiny_send.at[10]),
        pltpu.make_async_copy(sums.at[2], small_hbm.at[SECTIONS], tiny_send.at[11]),
    ]

    def tiny_0():
        for d in (1, 2, 3):
            tiny(0, d).start()

    def tiny_1():
        for d in (1, 2, 3):
            tiny(0, d).wait()
        sums[0] = (small[...] + sx[0]) + (sx[1] + sx[2])
        for d in (1, 2, 3):
            tiny(1, d).start()

    def tiny_2():
        for d in (1, 2, 3):
            tiny(1, d).wait()
        sums[1] = (sums[0] + sy[0]) + (sy[1] + sy[2])
        tiny(2, 1).start()

    def tiny_3():
        tiny(2, 1).wait()
        sums[2] = sums[1] + ss[...]
        for copy in keep_own:
            copy.start()
        for d in (1, 2, 3):
            tiny(3, d).start()

    def slot(t, carry):
        for number, turn in enumerate((tiny_0, tiny_1, tiny_2, tiny_3)):
            pl.when(t == number)(turn)
        for s in ORDER:
            k = t - OFFSET[s]
            live = (k >= 0) & (k < CHUNKS)
            if s < 5:
                live = live & ((parity == 1) | (k >= 4))
            elif s == 5:
                live = live & ((parity == 1) | (k < 2) | (k >= 4))
            else:
                live = live & (((parity == 1) & (k >= 2)) | ((parity == 0) & ((k < 2) | (k >= 4))))
            pl.when(live)(lambda turn=stages[s], k=k: turn(k))
        return carry

    lax.fori_loop(0, CHUNKS + max(OFFSET), slot, 0)

    for d in (1, 2, 3):
        tiny(3, d).wait()
    for copy in keep_own:
        copy.wait()

    @pl.when(parity == 1)
    def _():
        for k in range(2):
            for h in (0, 1):
                z_copy(k, h).wait_send()

    @pl.when(jnp.logical_not(last))
    def _():
        for micro in range(SLOTS):
            fwd_copy(micro).wait_send()

    @pl.when(jnp.logical_not(first))
    def _():
        for micro in range(SLOTS):
            bwd_copy(micro).wait_send()
            ig_copy(micro, 1).wait_recv()

    @pl.when(first)
    def _():
        for micro in range(SLOTS):
            ig_own(micro).wait()
            for d in (1, 2, 3):
                ig_copy(micro, d).wait_send()


def mega(block, cot, group_ids, live_count, group_scale, gains, shifts, qv_bias, up_bias, out_bias, w1, down):
    any_space = pl.BlockSpec(memory_space=pl.ANY)
    dma = pltpu.SemaphoreType.DMA
    return pl.pallas_call(
        mega_kernel,
        name="mega",
        out_shape=[
            jax.ShapeDtypeStruct((6 * 1024, WIDTH), BF16),
            jax.ShapeDtypeStruct((SECTIONS + 1, 16, WIDTH), F32),
            jax.ShapeDtypeStruct((SLOTS, LEN, 256), BF16),
        ],
        in_specs=[any_space] * 12,
        out_specs=[any_space, any_space, any_space],
        scratch_shapes=[
            pltpu.SMEM((SLOTS,), jnp.int32),
            pltpu.SMEM((1,), jnp.int32),
            pltpu.SMEM((8,), F32),
            pltpu.VMEM((1, 2, WIDTH), F32),
            pltpu.VMEM((1, 2, WIDTH), F32),
            pltpu.VMEM((2, 2, WIDTH), F32),
            pltpu.VMEM((2, FF), F32),
            pltpu.VMEM((1, WIDTH), F32),
            pltpu.VMEM((WIDTH, FF), BF16),
            pltpu.VMEM((2 * FF, WIDTH), BF16),
            pltpu.VMEM((WIDTH, FF), BF16),
            pltpu.VMEM((10, SLOTS, LEN, WIDTH), BF16),
            pltpu.VMEM((SLOTS, LEN, WIDTH), BF16),
            pltpu.VMEM((SLOTS, LEN, 1), F32),
            pltpu.VMEM((SLOTS, LEN, WIDTH), BF16),
            pltpu.VMEM((SLOTS, LEN, WIDTH), BF16),
            pltpu.VMEM((SLOTS, LEN, WIDTH), BF16),
            pltpu.VMEM((SLOTS, LEN, WIDTH), BF16),
            pltpu.VMEM((LEN, WIDTH), F32),
            pltpu.VMEM((16, WIDTH), F32),
            pltpu.VMEM((16, WIDTH), F32),
            pltpu.VMEM((2, 512, WIDTH), BF16),
            pltpu.VMEM((CHUNKS, 2, 2, 64, 512), BF16),
            pltpu.VMEM((CHUNKS, 2, 2, 64, WIDTH), BF16),
            pltpu.VMEM((CHUNKS, 2, 2, 16, 512), BF16),
            pltpu.VMEM((CHUNKS, 2, 2, 16, WIDTH), BF16),
            pltpu.VMEM((2, 2, 16, WIDTH), BF16),
            pltpu.VMEM((3, 16, WIDTH), F32),
            pltpu.VMEM((3, 16, WIDTH), F32),
            pltpu.VMEM((16, WIDTH), F32),
            pltpu.VMEM((3, 16, WIDTH), F32),
            dma((12,)), dma((2,)), dma((2,)), dma((20,)), dma((20,)),
            dma((SLOTS,)), dma((SLOTS,)), dma((SLOTS,)), dma((SLOTS,)),
            dma((SLOTS, 4)), dma((SLOTS,)),
            dma((CHUNKS,)), dma((CHUNKS,)), pltpu.SemaphoreType.REGULAR,
            dma((8, CHUNKS, 2, 2)), dma((8, CHUNKS, 2, 2)),
            dma((2, 2)), dma((2, 2)), dma((CHUNKS, 2)), dma((CHUNKS,)), dma((CHUNKS,)),
            dma((12,)), dma((12,)),
        ],
        compiler_params=pltpu.CompilerParams(
            collective_id=0, has_side_effects=True, vmem_limit_bytes=63 * 2**20
        ),
    )(block, cot, group_ids, live_count, group_scale, gains, shifts, qv_bias, up_bias, out_bias, w1, down)


def widen_kernel(
    reduced, sums_hbm, grad_in,
    first_out, down_out, qv_out, up_out, bias_out, gain_out, shift_out, grad_out,
    narrow, wide, sums, qv, up, bias, gain, shift, in_sem, out_sem, small_sem,
):
    rows, depth = wide.shape[1], wide.shape[0]
    count = 6 * 1024 // rows

    def load(i):
        return pltpu.make_async_copy(reduced.at[pl.ds(i * rows, rows)], narrow.at[i % depth], in_sem.at[i % depth])

    def store(i):
        chunk, cut = i * rows // 1024, pl.ds(i * rows % 1024, rows)
        if chunk < 2:
            target = down_out.at[pl.ds(i * rows, rows)]
        else:
            target = first_out.at[0, cut, pl.ds((chunk - 2) * 1024, 1024)]
        return pltpu.make_async_copy(wide.at[i % depth], target, out_sem.at[i % depth])

    for i in range(depth):
        load(i).start()
    load_sums = pltpu.make_async_copy(sums_hbm, sums, small_sem.at[0])
    load_sums.start()
    move_grad = pltpu.make_async_copy(grad_in, grad_out, small_sem.at[1])
    move_grad.start()
    small = [(qv, qv_out), (up, up_out), (bias, bias_out), (gain, gain_out), (shift, shift_out)]
    small = [pltpu.make_async_copy(*piece, small_sem.at[2 + j]) for j, piece in enumerate(small)]
    for i in range(count):
        load(i).wait()
        if i >= depth:
            store(i - depth).wait()
        wide[i % depth] = narrow[i % depth].astype(F32)
        store(i).start()
        if i + depth < count:
            load(i + depth).start()
        if i == 2:
            load_sums.wait()
            for layer in (0, 1):
                qv[layer, 0:1, :] = sums[2 * layer, 5:6, :]
                qv[layer, 1:2, :] = sums[2 * layer, 7:8, :]
                for j in range(4):
                    up[layer : layer + 1, j * WIDTH : (j + 1) * WIDTH] = sums[2 * layer + 1, 5 + j : 6 + j, :]
            bias[...] = sums[SECTIONS, 4:5, :]
            gain[0] = sums[SECTIONS, 0:2, :]
            shift[0] = sums[SECTIONS, 2:4, :]
            for copy in small:
                copy.start()
    for i in range(count - depth, count):
        store(i).wait()
    for copy in small:
        copy.wait()
    move_grad.wait()


def widen(reduced, sums, grad):
    any_space = pl.BlockSpec(memory_space=pl.ANY)
    rows, depth = 512, 4
    dma = pltpu.SemaphoreType.DMA
    shapes = [(2, 2, WIDTH), (2, FF), (1, WIDTH), (1, 2, WIDTH), (1, 2, WIDTH)]
    return pl.pallas_call(
        widen_kernel,
        name="widen",
        out_shape=[
            jax.ShapeDtypeStruct((1, WIDTH, FF), F32),
            jax.ShapeDtypeStruct((2 * WIDTH, WIDTH), F32),
            *[jax.ShapeDtypeStruct(shape, F32) for shape in shapes],
            jax.ShapeDtypeStruct((SLOTS, LEN, 256), BF16),
        ],
        in_specs=[any_space] * 3,
        out_specs=[any_space] * 8,
        scratch_shapes=[
            pltpu.VMEM((depth, rows, WIDTH), BF16),
            pltpu.VMEM((depth, rows, WIDTH), F32),
            pltpu.VMEM((SECTIONS + 1, 16, WIDTH), F32),
            *[pltpu.VMEM(shape, F32) for shape in shapes],
            dma((depth,)), dma((depth,)), dma((7,)),
        ],
        compiler_params=pltpu.CompilerParams(vmem_limit_bytes=48 * 2**20),
    )(reduced, sums, grad)


def on_device(
    block_input, cotangent, group_ids, live_count, group_scale, norm_gain, norm_bias, first_weight,
    qv_bias, up_bias, down_weight, out_bias,
):
    reduced, sums, grad = mega(
        block_input, cotangent, group_ids, live_count, group_scale, norm_gain, norm_bias,
        qv_bias, up_bias, out_bias, first_weight, down_weight,
    )
    first_grad, down_grad, qv_grad, up_grad, bias_grad, gain_grad, shift_grad, input_grad = widen(reduced, sums, grad)
    return input_grad, first_grad, down_grad, qv_grad, up_grad, bias_grad, gain_grad, shift_grad


def solution(mesh):
    in_specs = (
        P("dp", None, None),
        P("dp", None, None),
        P("dp"),
        P("dp"),
        P(),
        P("section", None, None),
        P("section", None, None),
        P("section", None, None),
        P(),
        P(),
        P("section", None),
        P("section", None),
    )
    out_specs = (
        P("dp", None, "section"),
        P("section", None, None),
        P("section", None),
        P(),
        P(),
        P("section", None),
        P("section", None, None),
        P("section", None, None),
    )
    return jax.shard_map(on_device, mesh=mesh, in_specs=in_specs, out_specs=out_specs, check_vma=False)
```

time: 1250 us -> 213 us (0.17)
  waiting for transfers between devices: 470 us -> 0 us
  Pallas kernels: 0 us -> 207 us
  matrix products: 204 us -> 0 us
  blocking collectives: 194 us -> 0 us
  other arithmetic: 147 us -> 0 us
  local copies, waits for them, and re-layouts: 98.9 us -> 1.92 us
  starting transfers between devices: 61.2 us -> 0 us
  loops' own time: 51.9 us -> 0 us
  between operations: 17.3 us -> 1.46 us
    ppermute x14 -> x0, waiting for transfers between devices: 239 us -> none  [passed_along(): lax.ppermute(value, axis, [(source, source + steps) for source in range(i...]
    psum x1 -> x0, waiting for transfers between devices: 231 us -> none  [on_device(): lax.psum(first_sum.astype(jnp.bfloat16), 'dp').astype(jnp.float32)]
    pallas_call x0 -> x2, Pallas kernels: none -> 207 us  [the longest x1 195 us: mega(): pl.pallas_call(mega_kernel, name='mega', out_shape=[jax.ShapeDtypeStruct(...]
    dot_general x24 -> x0, matrix products: 204 us -> none  [the longest x8 115 us: contract_rows(): lax.dot_general(left_side, right_side, (((0,), (0,)), ((), ())), preferre...]
    psum x2 -> x0, blocking collectives: 194 us -> none  [the longest x1 124 us: on_device(): lax.psum(branch_sum.astype(jnp.bfloat16), 'dp').astype(jnp.float32)]
    ppermute x14 -> x0, starting transfers between devices: 61.1 us -> none  [passed_along(): lax.ppermute(value, axis, [(source, source + steps) for source in range(i...]
    another operation x22 -> x0, loops' own time: 51.9 us -> none  [the longest x7 37.1 us: on_device(): lax.cond(running, backward_run, backward_spare, (carried, clipped, incomi...]
    dynamic_update_slice x41 -> x0, other arithmetic: 43.8 us -> none  [place_slot(): lax.dynamic_update_index_in_dim(buffer, jnp.where(running, entries, previ...]
  transfers between devices with their start and end apart: 16 -> 0, of which waited for: 12 -> 0; matrix products, arithmetic and copies ran while one was open for 8% -> 0% of each run, Pallas kernels for 0% -> 0%
where the time goes in v1:
time: 213 us; the launch traced here: 211 us
  Pallas kernels  207 us (97%)
    pallas_call x1, Pallas kernels, mega(): pl.pallas_call(mega_kernel, name='mega', out_shape=[jax.ShapeDtypeStruct(...  195 us
    pallas_call x1, Pallas kernels, widen(): pl.pallas_call(widen_kernel, name='widen', out_shape=[jax.ShapeDtypeStruc...  12.3 us

profile of v1, /device:TPU:33, one launch (start us, length us, event | category | flops | bytes accessed | tf_op | source)
XLA Modules:
  0.0 210.7 jit_solution(13481432261738264479)
XLA Ops:
  1.3 195.0 %mega.1 = (bf16[6144,1024]{1,0:T(8,128)(2,1)}, f32[5,16,1024]{2,1,0:T(8,128)}, bf16[4,128,256]{2,1,0:T(8,128)(2,1)}) custom-call(bf16[4,128,1024]{2,1,0:T(8,128)(2,1)} %block_hbm.1, bf16[4,128,1024]{2,1,0:T(8,128)(2,1)} %cot_hbm.1, s32[4]{0:T(128)} %group_hbm.1, s32[1]{0:T(128)S(6)} %copy.20.live_hbm, f32[8]{0:T(128)} %scale_hbm.1, f32[1,2,1024]{2,1,0:T(2,128)} %gains_hbm.1, ...), custom_call_target="tpu_custom_call" | custom-call | tf_op jit(solution)/shard_map/mega/pallas_call | solution.py:749
  196.3 0.0 copy-start
  196.3 1.0 copy-done
  197.2 0.0 copy-start.1
  197.2 0.9 copy-done.1
  198.2 12.3 %widen.1 = (f32[1,1024,4096]{2,1,0:T(8,128)}, f32[2048,1024]{1,0:T(8,128)}, f32[2,2,1024]{2,1,0:T(2,128)}, f32[2,4096]{1,0:T(2,128)}, f32[1,1024]{1,0:T(1,128)},...) custom-call(bf16[6144,1024]{1,0:T(8,128)(2,1)} %get-tuple-element.19.reduced, ...), custom_call_target="tpu_custom_call" | custom-call | tf_op jit(solution)/shard_map/widen/pallas_call | solution.py:864
Async XLA Ops:
  196.3 1.0 copy-start
  197.2 0.9 copy-start.1

commit v2 on v1

--- a/solution.py
+++ b/solution.py
@@ -21,8 +21,9 @@
 NORM_EPS = 1e-05
 GELU_C = math.sqrt(2.0 / math.pi)
 CHUNKS = 8
-ORDER = (10, 0, 8, 3, 4, 5, 1, 9, 6, 7, 2)
-OFFSET = (0, 1, 2, 4, 5, 6, 7, 8, 11, 13, 20)
+ORDER = (0, 3, 4, 5, 8, 9, 1, 6, 7, 2)
+OFFSET_FEED = (0, 1, 2, 4, 5, 6, 7, 8, 11, 13)
+OFFSET_ATTEND = (0, 1, 5, 7, 8, 9, 10, 11, 14, 16)
 
 
 def device(section, x, y, core):
@@ -236,15 +237,19 @@
     def _():
         load_cot.wait()
 
-    def fwd_copy(micro):
+    halves = (pl.ds(0, LEN // 2), pl.ds(LEN // 2, LEN // 2))
+
+    def fwd_copy(micro, half):
+        rows = halves[half]
         return remote(
-            r_out.at[micro], r_in.at[micro], fwd_send.at[micro], fwd_recv.at[micro],
+            r_out.at[micro, rows], r_in.at[micro, rows], fwd_send.at[micro, half], fwd_recv.at[micro, half],
             device((section + 1) % 4, x, y, core),
         )
 
-    def bwd_copy(micro):
+    def bwd_copy(micro, half):
+        rows = halves[half]
         return remote(
-            g_out.at[micro], g_in.at[micro], bwd_send.at[micro], bwd_recv.at[micro],
+            g_out.at[micro, rows], g_in.at[micro, rows], bwd_send.at[micro, half], bwd_recv.at[micro, half],
             device((section + 3) % 4, x, y, core),
         )
 
@@ -362,13 +367,15 @@
         wide[...] = total
 
     def forward(micro):
-        @pl.when(jnp.logical_not(first))
-        def _():
-            fwd_copy(micro).wait_recv()
-
-        residual = r_in[micro].astype(F32)
-        unit, _ = normalize(residual)
-        ops[0, micro] = (unit * gains[0, 0:1, :] + shifts[0, 0:1, :]).astype(BF16)
+        for half in (0, 1):
+            rows = halves[half]
+
+            @pl.when(jnp.logical_not(first))
+            def _():
+                fwd_copy(micro, half).wait_recv()
+
+            unit, _ = normalize(r_in[micro, rows].astype(F32))
+            ops[0, micro, rows] = (unit * gains[0, 0:1, :] + shifts[0, 0:1, :]).astype(BF16)
 
         @pl.when(parity == 0)
         def _():
@@ -378,27 +385,30 @@
         def _():
             feed_forward(micro)
 
-        unit, inverse = normalize(wide[...])
-        units[micro] = unit.astype(BF16)
-        inverses[micro] = inverse
-
-        @pl.when(jnp.logical_not(last))
-        def _():
-            r_out[micro] = (r_in[micro].astype(F32) + unit * gains[0, 1:2, :] + shifts[0, 1:2, :]).astype(BF16)
-            fwd_copy(micro).start()
+        for half in (0, 1):
+            rows = halves[half]
+            unit, inverse = normalize(wide[rows])
+            units[micro, rows] = unit.astype(BF16)
+            inverses[micro, rows] = inverse
+
+            @pl.when(jnp.logical_not(last))
+            def _():
+                after = r_in[micro, rows].astype(F32) + unit * gains[0, 1:2, :] + shifts[0, 1:2, :]
+                r_out[micro, rows] = after.astype(BF16)
+                fwd_copy(micro, half).start()
 
     def backward(micro):
-        @pl.when(jnp.logical_not(last))
-        def _():
-            bwd_copy(micro).wait_recv()
-
-        incoming = g_in[micro].astype(F32) * sequence_weight(micro)
-        unit = units[micro].astype(F32)
-        small[1:2, :] += column_sum(incoming * unit)
-        small[3:4, :] += column_sum(incoming)
-        grad_branch = norm_backward(incoming, unit, inverses[micro], gains[0, 1:2, :]).astype(BF16)
-        ops[1, micro] = grad_branch
-        small[4:5, :] += column_sum(grad_branch.astype(F32))
+        weight = sequence_weight(micro)
+        for half in (0, 1):
+            rows = halves[half]
+
+            @pl.when(jnp.logical_not(last))
+            def _():
+                bwd_copy(micro, half).wait_recv()
+
+            incoming = g_in[micro, rows].astype(F32) * weight
+            unit = units[micro, rows].astype(F32)
+            ops[1, micro, rows] = norm_backward(incoming, unit, inverses[micro, rows], gains[0, 1:2, :]).astype(BF16)
 
         @pl.when(parity == 0)
         def _():
@@ -408,23 +418,33 @@
         def _():
             feed_backward(micro)
 
-        grad_normed = wide[...]
-        unit, inverse = normalize(r_in[micro].astype(F32))
-        small[0:1, :] += column_sum(grad_normed * unit)
-        small[2:3, :] += column_sum(grad_normed)
-        incoming = g_in[micro].astype(F32) * sequence_weight(micro)
-        grad = incoming + norm_backward(grad_normed, unit, inverse, gains[0, 0:1, :])
-        g_out[micro] = grad.astype(BF16)
-
-        @pl.when(jnp.logical_not(first))
-        def _():
-            bwd_copy(micro).start()
+        units_pre = []
+        for half in (0, 1):
+            rows = halves[half]
+            unit, inverse = normalize(r_in[micro, rows].astype(F32))
+            units_pre.append(unit)
+            incoming = g_in[micro, rows].astype(F32) * weight
+            grad = incoming + norm_backward(wide[rows], unit, inverse, gains[0, 0:1, :])
+            g_out[micro, rows] = grad.astype(BF16)
+
+            @pl.when(jnp.logical_not(first))
+            def _():
+                bwd_copy(micro, half).start()
 
         @pl.when(first)
         def _():
             ig_own(micro).start()
             for d in (1, 2, 3):
                 ig_copy(micro, d).start()
+
+        for half in (0, 1):
+            rows = halves[half]
+            incoming = g_in[micro, rows].astype(F32) * weight
+            small[0:1, :] += column_sum(wide[rows] * units_pre[half])
+            small[1:2, :] += column_sum(incoming * units[micro, rows].astype(F32))
+            small[2:3, :] += column_sum(wide[rows])
+            small[3:4, :] += column_sum(incoming)
+            small[4:5, :] += column_sum(ops[1, micro, rows].astype(F32))
 
     turn_at = jnp.where(section >= 2, 0, SLOTS)
 
@@ -456,86 +476,96 @@
             return device(section, (x + d) % 4, y, core)
         return device(section, x, (y + d) % 4, core)
 
-    def at(k, h, b1, b2, n, c=None):
+    def chunk(q):
+        return jnp.where(parity == 1, q, jnp.where(q < 4, q + 4, q - 4))
+
+    def at(q, h, b1, b2, n, c=None):
         c = core if c is None else c
-        row = k * 1024 + c * 512 + h * 256 + b1 * 64 + b2 * 16
+        row = chunk(q) * 1024 + c * 512 + h * 256 + b1 * 64 + b2 * 16
         return pl.ds(pl.multiple_of(row, 16), n)
 
-    def out_chunk(k):
-        return jnp.where(parity == 1, k - 2, jnp.where(k < 2, k, k - 2))
+    def out_at(q, h, b1, b2, n):
+        k = chunk(q)
+        k = jnp.where((parity == 1) | (k >= 4), k - 2, k)
+        row = k * 1024 + core * 512 + h * 256 + b1 * 64 + b2 * 16
+        return pl.ds(pl.multiple_of(row, 16), n)
 
     left, right = pl.ds(0, 512), pl.ds(512, 512)
-
-    def ring(stage, k, h, d, source, target, to):
-        return remote(source, target, ring_send.at[stage, k, h, d], ring_recv.at[stage, k, h, d], to)
-
-    def pair_copy(k):
-        rows = at(k, 0, 0, 0, 512, 1 - core)
-        return remote(buffer.at[rows], pair.at[k % 2], pair_send.at[k], pair_recv.at[k], sibling)
-
-    def rs_one(k, h, d):
+    both = [(h, d) for h in (0, 1) for d in (0, 1)]
+
+    def ring(stage, q, source, target, to):
+        return remote(source, target, ring_send.at[stage // 4], ring_recv.at[stage, q], to)
+
+    def arrived(like, sem):
+        pltpu.make_async_copy(like, like, sem).wait()
+
+    def pair_copy(q):
+        rows = at(q, 0, 0, 0, 512, 1 - core)
+        return remote(buffer.at[rows], pair.at[q % 2], pair_send, pair_recv.at[q % 2], sibling)
+
+    def rs_one(q, h, d):
         p1, _ = spot(h)
-        rows = at(k, h, (p1 + 2) % 4, 0, 64)
-        return ring(0, k, h, d, buffer.at[rows, left if d == 0 else right], r1.at[k, h, d], peer(h, 1 - 2 * d))
-
-    def rs_two(k, h, d):
+        rows = at(q, h, (p1 + 2) % 4, 0, 64)
+        return ring(0, q, buffer.at[rows, left if d == 0 else right], r1.at[q, h, d], peer(h, 1 - 2 * d))
+
+    def rs_two(q, h, d):
         p1, _ = spot(h)
         step = 1 - 2 * d
-        return ring(1, k, h, d, buffer.at[at(k, h, (p1 + step) % 4, 0, 64)], r2.at[k, h, d], peer(h, step))
-
-    def rs_three(k, h, d):
+        return ring(1, q, buffer.at[at(q, h, (p1 + step) % 4, 0, 64)], r2.at[q, h, d], peer(h, step))
+
+    def rs_three(q, h, d):
         p1, p2 = spot(h)
-        rows = at(k, h, p1, (p2 + 2) % 4, 16)
-        return ring(2, k, h, d, buffer.at[rows, left if d == 0 else right], r3.at[k, h, d], peer(1 - h, 1 - 2 * d))
-
-    def rs_four(k, h, d):
+        rows = at(q, h, p1, (p2 + 2) % 4, 16)
+        return ring(2, q, buffer.at[rows, left if d == 0 else right], r3.at[q, h, d], peer(1 - h, 1 - 2 * d))
+
+    def rs_four(q, h, d):
         p1, p2 = spot(h)
         step = 1 - 2 * d
-        return ring(3, k, h, d, buffer.at[at(k, h, p1, (p2 + step) % 4, 16)], r4.at[k, h, d], peer(1 - h, step))
+        return ring(3, q, buffer.at[at(q, h, p1, (p2 + step) % 4, 16)], r4.at[q, h, d], peer(1 - h, step))
 
     def z_copy(k, h):
         p1, p2 = spot(h)
+        row = k * 1024 + core * 512 + h * 256 + p1 * 64 + p2 * 16
         return remote(
-            buffer.at[at(k, h, p1, p2, 16)], z.at[k, h], z_send.at[k, h], z_recv.at[k, h],
+            buffer.at[pl.ds(pl.multiple_of(row, 16), 16)], z.at[k, h], z_send, z_recv.at[k, h],
             device((section + 3) % 4, x, y, core),
         )
 
-    def own_copy(k, h):
+    def own_copy(q, h):
         p1, p2 = spot(h)
         return pltpu.make_async_copy(
-            buffer.at[at(k, h, p1, p2, 16)], out_hbm.at[at(out_chunk(k), h, p1, p2, 16)], own_sem.at[k, h]
+            buffer.at[at(q, h, p1, p2, 16)], out_hbm.at[out_at(q, h, p1, p2, 16)], own_sem.at[q]
         )
 
-    def ag_one(k, h, d):
+    def ag_one(q, h, d):
         p1, p2 = spot(h)
-        return ring(
-            4, k, h, d, buffer.at[at(k, h, p1, p2, 16)], out_hbm.at[at(out_chunk(k), h, p1, p2, 16)], peer(1 - h, 1 - 2 * d)
-        )
-
-    def ag_two(k, h, d):
+        target = out_hbm.at[out_at(q, h, p1, p2, 16)]
+        return ring(4, q, buffer.at[at(q, h, p1, p2, 16)], target, peer(1 - h, 1 - 2 * d))
+
+    def ag_two(q, h, d):
         p1, p2 = spot(h)
         step = 1 - 2 * d
-        piece = out_hbm.at[at(out_chunk(k), h, p1, (p2 - step) % 4, 16), left if d == 0 else right]
-        return ring(5, k, h, d, piece, piece, peer(1 - h, step))
-
-    def ag_three(k, h, d):
+        piece = out_hbm.at[out_at(q, h, p1, (p2 - step) % 4, 16), left if d == 0 else right]
+        return ring(5, q, piece, piece, peer(1 - h, step))
+
+    def ag_three(q, h, d):
         p1, _ = spot(h)
-        piece = out_hbm.at[at(out_chunk(k), h, p1, 0, 64)]
-        return ring(6, k, h, d, piece, piece, peer(h, 1 - 2 * d))
-
-    def ag_four(k, h, d):
+        piece = out_hbm.at[out_at(q, h, p1, 0, 64)]
+        return ring(6, q, piece, piece, peer(h, 1 - 2 * d))
+
+    def ag_four(q, h, d):
         p1, _ = spot(h)
         step = 1 - 2 * d
-        piece = out_hbm.at[at(out_chunk(k), h, (p1 - step) % 4, 0, 64), left if d == 0 else right]
-        return ring(7, k, h, d, piece, piece, peer(h, step))
-
-    def last_copy(k):
-        piece = out_hbm.at[at(out_chunk(k), 0, 0, 0, 512)]
-        return remote(piece, piece, last_send.at[k], last_recv.at[k], sibling)
-
-    both = [(h, d) for h in (0, 1) for d in (0, 1)]
-
-    def stage_0(k):
+        piece = out_hbm.at[out_at(q, h, (p1 - step) % 4, 0, 64), left if d == 0 else right]
+        return ring(7, q, piece, piece, peer(h, step))
+
+    def last_copy(q, h, d):
+        p1, _ = spot(h)
+        piece = out_hbm.at[out_at(q, h, (p1 + d) % 4, 0, 64)]
+        return remote(piece, piece, last_send, last_recv, sibling)
+
+    def stage_0(q):
+        k = chunk(q)
         feed_down = (parity == 1) & (k < 4)
         from_context = (parity == 0) & (k == 7)
         a = jnp.where(feed_down, 2 + k, jnp.where(from_context, 1, 0))
@@ -545,114 +575,105 @@
             left_side = ops[a, :, :, cut * 256 : (cut + 1) * 256].reshape(ROWS, 256)
             product = dot_tn(left_side, right_side)
             buffer[pl.ds(pl.multiple_of(k * 1024 + cut * 256, 256), 256), :] = product.astype(BF16)
-        pl.when(k >= 6 - 4 * parity)(lambda: pl.semaphore_wait(pair_free, 1))
-        pair_copy(k).start()
-
-    def stage_1(k):
-        pair_copy(k).wait()
-        rows = at(k, 0, 0, 0, 512)
-        buffer[rows, :] = buffer[rows, :] + pair[k % 2]
-
-        @pl.when(k < CHUNKS - 2)
+        pl.when(q >= 2)(lambda: pl.semaphore_wait(pair_free, 1))
+        pair_copy(q).start()
+
+    def stage_1(q):
+        pair_copy(q).wait_recv()
+        rows = at(q, 0, 0, 0, 512)
+        buffer[rows, :] = buffer[rows, :] + pair[q % 2]
+
+        @pl.when(q < 2 + 4 * parity)
         def _():
             pl.semaphore_signal(pair_free, inc=1, device_id=sibling, device_id_type=MESH)
 
         for h, d in both:
-            rs_one(k, h, d).start()
-
-    def stage_2(k):
+            rs_one(q, h, d).start()
+
+    def stage_2(q):
+        arrived(r1.at[q], ring_recv.at[0, q])
         for h, d in both:
-            rs_one(k, h, d).wait()
             p1, _ = spot(h)
-            rows = at(k, h, (p1 + 1 - 2 * d) % 4, 0, 64)
+            rows = at(q, h, (p1 + 1 - 2 * d) % 4, 0, 64)
             cut = left if d == 0 else right
-            buffer[rows, cut] = buffer[rows, cut] + r1[k, h, d]
-            rs_two(k, h, d).start()
-
-    def stage_3(k):
+            buffer[rows, cut] = buffer[rows, cut] + r1[q, h, d]
+            rs_two(q, h, d).start()
+
+    def stage_3(q):
+        arrived(r2.at[q], ring_recv.at[1, q])
         for h in (0, 1):
             p1, _ = spot(h)
-            for d in (0, 1):
-                rs_two(k, h, d).wait()
-            rows = at(k, h, p1, 0, 64)
-            total = buffer[rows, :].astype(F32) + r2[k, h, 0].astype(F32) + r2[k, h, 1].astype(F32)
+            rows = at(q, h, p1, 0, 64)
+            total = buffer[rows, :].astype(F32) + r2[q, h, 0].astype(F32) + r2[q, h, 1].astype(F32)
             buffer[rows, :] = total.astype(BF16)
             for d in (0, 1):
-                rs_three(k, h, d).start()
-
-    def stage_4(k):
+                rs_three(q, h, d).start()
+
+    def stage_4(q):
+        arrived(r3.at[q], ring_recv.at[2, q])
         for h, d in both:
-            rs_three(k, h, d).wait()
             p1, p2 = spot(h)
-            rows = at(k, h, p1, (p2 + 1 - 2 * d) % 4, 16)
+            rows = at(q, h, p1, (p2 + 1 - 2 * d) % 4, 16)
             cut = left if d == 0 else right
-            buffer[rows, cut] = buffer[rows, cut] + r3[k, h, d]
-            rs_four(k, h, d).start()
-
-    def spread(k):
-        for h in (0, 1):
-            own_copy(k, h).start()
-            for d in (0, 1):
-                ag_one(k, h, d).start()
-
-    def stage_5(k):
-        @pl.when((parity == 1) | (k >= 4))
-        def _():
+            buffer[rows, cut] = buffer[rows, cut] + r3[q, h, d]
+            rs_four(q, h, d).start()
+
+    def stage_5(q):
+        @pl.when((parity == 1) | (q < 4))
+        def _():
+            arrived(r4.at[q], ring_recv.at[3, q])
             for h in (0, 1):
                 p1, p2 = spot(h)
-                for d in (0, 1):
-                    rs_four(k, h, d).wait()
-                rows = at(k, h, p1, p2, 16)
-                total = buffer[rows, :].astype(F32) + r4[k, h, 0].astype(F32) + r4[k, h, 1].astype(F32)
+                rows = at(q, h, p1, p2, 16)
+                total = buffer[rows, :].astype(F32) + r4[q, h, 0].astype(F32) + r4[q, h, 1].astype(F32)
                 buffer[rows, :] = total.astype(BF16)
 
-        @pl.when((parity == 1) & (k < 2))
+        @pl.when((parity == 1) & (q < 2))
         def _():
             for h in (0, 1):
-                z_copy(k, h).start()
-
-        @pl.when((parity == 0) & (k < 2))
+                z_copy(q, h).start()
+
+        @pl.when((parity == 0) & (q >= 4))
         def _():
             for h in (0, 1):
                 p1, p2 = spot(h)
-                z_copy(k, h).wait_recv()
-                buffer[at(k, h, p1, p2, 16), :] = z[k, h]
-
-        @pl.when(((parity == 1) & (k >= 2)) | (parity == 0))
-        def _():
-            spread(k)
-
-    def stage_6(k):
+                z_copy(q - 4, h).wait_recv()
+                buffer[at(q, h, p1, p2, 16), :] = z[q - 4, h]
+
+        @pl.when((parity == 0) | (q >= 2))
+        def _():
+            for h in (0, 1):
+                own_copy(q, h).start()
+                for d in (0, 1):
+                    ag_one(q, h, d).start()
+
+    def stage_6(q):
+        arrived(r4.at[q], ring_recv.at[4, q])
+        for h, d in both:
+            ag_two(q, h, d).start()
+        arrived(r3.at[q], own_sem.at[q])
+
+    def stage_7(q):
+        arrived(r3.at[q], ring_recv.at[5, q])
+        for h, d in both:
+            ag_three(q, h, d).start()
         for h in (0, 1):
-            for d in (0, 1):
-                ag_one(k, h, d).wait()
-            for d in (0, 1):
-                ag_two(k, h, d).start()
-            own_copy(k, h).wait()
-
-    def stage_7(k):
+            last_copy(q, h, 0).start()
+
+    def stage_8(q):
+        arrived(r2.at[q], ring_recv.at[6, q])
+        for h, d in both:
+            ag_four(q, h, d).start()
         for h in (0, 1):
-            for d in (0, 1):
-                ag_two(k, h, d).wait()
-            for d in (0, 1):
-                ag_three(k, h, d).start()
-
-    def stage_8(k):
+            last_copy(q, h, 1).start()
+            last_copy(q, h, 3).start()
+
+    def stage_9(q):
+        arrived(r1.at[q], ring_recv.at[7, q])
         for h in (0, 1):
-            for d in (0, 1):
-                ag_three(k, h, d).wait()
-            for d in (0, 1):
-                ag_four(k, h, d).start()
-
-    def stage_9(k):
-        for h, d in both:
-            ag_four(k, h, d).wait()
-        last_copy(k).start()
-
-    def stage_10(k):
-        last_copy(k).wait()
-
-    stages = [stage_0, stage_1, stage_2, stage_3, stage_4, stage_5, stage_6, stage_7, stage_8, stage_9, stage_10]
+            last_copy(q, h, 2).start()
+
+    stages = [stage_0, stage_1, stage_2, stage_3, stage_4, stage_5, stage_6, stage_7, stage_8, stage_9]
 
     def tiny(phase, d):
         if phase == 0:
@@ -700,39 +721,53 @@
         for number, turn in enumerate((tiny_0, tiny_1, tiny_2, tiny_3)):
             pl.when(t == number)(turn)
         for s in ORDER:
-            k = t - OFFSET[s]
+            k = t - jnp.where(parity == 1, OFFSET_FEED[s], OFFSET_ATTEND[s])
             live = (k >= 0) & (k < CHUNKS)
             if s < 5:
-                live = live & ((parity == 1) | (k >= 4))
+                live = live & ((parity == 1) | (k < 4))
             elif s == 5:
-                live = live & ((parity == 1) | (k < 2) | (k >= 4))
+                live = live & ((parity == 1) | (k < 6))
             else:
-                live = live & (((parity == 1) & (k >= 2)) | ((parity == 0) & ((k < 2) | (k >= 4))))
+                live = live & jnp.where(parity == 1, k >= 2, k < 6)
             pl.when(live)(lambda turn=stages[s], k=k: turn(k))
         return carry
 
-    lax.fori_loop(0, CHUNKS + max(OFFSET), slot, 0)
+    lax.fori_loop(0, CHUNKS + max(OFFSET_FEED + OFFSET_ATTEND), slot, 0)
 
     for d in (1, 2, 3):
         tiny(3, d).wait()
     for copy in keep_own:
         copy.wait()
 
+    def sent(rows, sem):
+        arrived(buffer.at[pl.ds(0, rows)], sem)
+
     @pl.when(parity == 1)
     def _():
-        for k in range(2):
-            for h in (0, 1):
-                z_copy(k, h).wait_send()
+        sent(8 * 512, pair_send)
+        sent(8 * 480, ring_send.at[0])
+        sent(2 * 32, z_send)
+
+    @pl.when(parity == 0)
+    def _():
+        sent(4 * 512, pair_send)
+        sent(4 * 480, ring_send.at[0])
+
+    sent(6 * 480, ring_send.at[1])
+    sent(6 * 512, last_send)
+    sent(6 * 512, last_recv)
 
     @pl.when(jnp.logical_not(last))
     def _():
         for micro in range(SLOTS):
-            fwd_copy(micro).wait_send()
+            for half in (0, 1):
+                fwd_copy(micro, half).wait_send()
 
     @pl.when(jnp.logical_not(first))
     def _():
         for micro in range(SLOTS):
-            bwd_copy(micro).wait_send()
+            for half in (0, 1):
+                bwd_copy(micro, half).wait_send()
             ig_copy(micro, 1).wait_recv()
 
     @pl.when(first)
@@ -789,11 +824,10 @@
             pltpu.VMEM((16, WIDTH), F32),
             pltpu.VMEM((3, 16, WIDTH), F32),
             dma((12,)), dma((2,)), dma((2,)), dma((20,)), dma((20,)),
-            dma((SLOTS,)), dma((SLOTS,)), dma((SLOTS,)), dma((SLOTS,)),
+            dma((SLOTS, 2)), dma((SLOTS, 2)), dma((SLOTS, 2)), dma((SLOTS, 2)),
             dma((SLOTS, 4)), dma((SLOTS,)),
-            dma((CHUNKS,)), dma((CHUNKS,)), pltpu.SemaphoreType.REGULAR,
-            dma((8, CHUNKS, 2, 2)), dma((8, CHUNKS, 2, 2)),
-            dma((2, 2)), dma((2, 2)), dma((CHUNKS, 2)), dma((CHUNKS,)), dma((CHUNKS,)),
+            dma, dma((2,)), pltpu.SemaphoreType.REGULAR,
+            dma((2,)), dma((8, CHUNKS)), dma, dma((2, 2)), dma((CHUNKS,)), dma, dma,
             dma((12,)), dma((12,)),
         ],
         compiler_params=pltpu.CompilerParams(
@@ -879,7 +913,7 @@
             *[pltpu.VMEM(shape, F32) for shape in shapes],
             dma((depth,)), dma((depth,)), dma((7,)),
         ],
-        compiler_params=pltpu.CompilerParams(vmem_limit_bytes=48 * 2**20),
+        compiler_params=pltpu.CompilerParams(vmem_limit_bytes=63 * 2**20),
     )(reduced, sums, grad)
 
 

time: 213 us -> 206 us (0.967)
  Pallas kernels: 207 us -> 204 us
    pallas_call x1, Pallas kernels: 195 us -> 192 us  [mega(): pl.pallas_call(mega_kernel, name='mega', out_shape=[jax.ShapeDtypeStruct(...]
where the time goes in v2:
time: 206 us; the launch traced here: 205 us
  Pallas kernels  204 us (99%)
    pallas_call x1, Pallas kernels, mega(): pl.pallas_call(mega_kernel, name='mega', out_shape=[jax.ShapeDtypeStruct(...  192 us
    pallas_call x1, Pallas kernels, widen(): pl.pallas_call(widen_kernel, name='widen', out_shape=[jax.ShapeDtypeStruc...  12.4 us

profile of v2, /device:TPU:33, one launch (start us, length us, event | category | flops | bytes accessed | tf_op | source)
XLA Modules:
  0.0 205.4 jit_solution(5715580644254044052)
XLA Ops:
  1.3 191.6 %mega.1 = (bf16[6144,1024]{1,0:T(8,128)(2,1)}, f32[5,16,1024]{2,1,0:T(8,128)}, bf16[4,128,256]{2,1,0:T(8,128)(2,1)}) custom-call(bf16[4,128,1024]{2,1,0:T(8,128)(2,1)} %block_hbm.1, bf16[4,128,1024]{2,1,0:T(8,128)(2,1)} %cot_hbm.1, s32[4]{0:T(128)} %group_hbm.1, s32[1]{0:T(128)S(6)} %copy.20.live_hbm, f32[8]{0:T(128)} %scale_hbm.1, f32[1,2,1024]{2,1,0:T(2,128)} %gains_hbm.1, ...), custom_call_target="tpu_custom_call" | custom-call | tf_op jit(solution)/shard_map/mega/pallas_call | solution.py:784
  192.9 12.4 %widen.1 = (f32[1,1024,4096]{2,1,0:T(8,128)}, f32[2048,1024]{1,0:T(8,128)}, f32[2,2,1024]{2,1,0:T(2,128)}, f32[2,4096]{1,0:T(2,128)}, f32[1,1024]{1,0:T(1,128)},...) custom-call(bf16[6144,1024]{1,0:T(8,128)(2,1)} %get-tuple-element.19.reduced, ...), custom_call_target="tpu_custom_call" | custom-call | tf_op jit(solution)/shard_map/widen/pallas_call | solution.py:898

commit v3 on v2

--- a/solution.py
+++ b/solution.py
@@ -21,9 +21,9 @@
 NORM_EPS = 1e-05
 GELU_C = math.sqrt(2.0 / math.pi)
 CHUNKS = 8
-ORDER = (0, 3, 4, 5, 8, 9, 1, 6, 7, 2)
-OFFSET_FEED = (0, 1, 2, 4, 5, 6, 7, 8, 11, 13)
-OFFSET_ATTEND = (0, 1, 5, 7, 8, 9, 10, 11, 14, 16)
+ORDER = (0, 3, 4, 5, 8, 9, 6, 7, 2)
+OFFSET_FEED = (0, 0, 1, 3, 4, 5, 6, 7, 10, 12)
+OFFSET_ATTEND = (0, 0, 4, 6, 7, 8, 9, 10, 13, 15)
 
 
 def device(section, x, y, core):
@@ -97,11 +97,11 @@
     block_hbm, cot_hbm, group_hbm, live_hbm, scale_hbm, gains_hbm, shifts_hbm, qv_hbm, up_hbm, bias_hbm, w1_hbm, down_hbm,
     out_hbm, small_hbm, grad_hbm,
     group_ids, live_count, group_scale, gains, shifts, qv_bias, up_bias, out_bias,
-    w1, buffer, w2t, ops, units, inverses, r_in, r_out, g_in, g_out, wide, small, vectors,
-    pair, r1, r2, r3, r4, z, sx, sy, ss, sums,
+    w1, buffer, w2t, ops, other, units, stats, r_in, r_out, g_in, g_out, wide, small, vectors,
+    z, sx, sy, ss, sums,
     load_sem, down_send, down_recv, ag_send, ag_recv,
     fwd_send, fwd_recv, bwd_send, bwd_recv, ig_send, ig_recv,
-    pair_send, pair_recv, pair_free, ring_send, ring_recv, z_send, z_recv, own_sem, last_send, last_recv,
+    swap_send, swap_recv, ready, ring_send, ring_recv, z_send, z_recv, own_sem, last_send, last_recv,
     tiny_send, tiny_recv,
 ):
     section, x, y, core = place()
@@ -237,19 +237,15 @@
     def _():
         load_cot.wait()
 
-    halves = (pl.ds(0, LEN // 2), pl.ds(LEN // 2, LEN // 2))
-
-    def fwd_copy(micro, half):
-        rows = halves[half]
+    def fwd_copy(micro):
         return remote(
-            r_out.at[micro, rows], r_in.at[micro, rows], fwd_send.at[micro, half], fwd_recv.at[micro, half],
+            r_out.at[micro], r_in.at[micro], fwd_send.at[micro], fwd_recv.at[micro],
             device((section + 1) % 4, x, y, core),
         )
 
-    def bwd_copy(micro, half):
-        rows = halves[half]
+    def bwd_copy(micro):
         return remote(
-            g_out.at[micro, rows], g_in.at[micro, rows], bwd_send.at[micro, half], bwd_recv.at[micro, half],
+            g_out.at[micro], g_in.at[micro], bwd_send.at[micro], bwd_recv.at[micro],
             device((section + 3) % 4, x, y, core),
         )
 
@@ -351,8 +347,6 @@
         for j in range(3):
             part = ops[6 + j, micro]
             total = total + dot(part, w1t[j * WIDTH : (j + 1) * WIDTH, :])
-            if j != 1:
-                small[5 + j : 6 + j, :] += column_sum(part.astype(F32))
         wide[...] = total
 
     def feed_backward(micro):
@@ -362,20 +356,26 @@
             grad = dot(grad_branch, w2t[:, j * WIDTH : (j + 1) * WIDTH])
             grad = (grad * ops[6 + j, micro].astype(F32)).astype(BF16)
             ops[6 + j, micro] = grad
-            small[5 + j : 6 + j, :] += column_sum(grad.astype(F32))
             total = total + dot(grad, w1t[j * WIDTH : (j + 1) * WIDTH, :])
         wide[...] = total
 
+    def swap(block, count, micro, group):
+        piece = pl.ds(block, count)
+        return remote(ops.at[piece, micro], other.at[piece, micro], swap_send, swap_recv.at[group], sibling)
+
     def forward(micro):
-        for half in (0, 1):
-            rows = halves[half]
-
-            @pl.when(jnp.logical_not(first))
-            def _():
-                fwd_copy(micro, half).wait_recv()
-
-            unit, _ = normalize(r_in[micro, rows].astype(F32))
-            ops[0, micro, rows] = (unit * gains[0, 0:1, :] + shifts[0, 0:1, :]).astype(BF16)
+        @pl.when(jnp.logical_not(first))
+        def _():
+            fwd_copy(micro).wait_recv()
+
+        residual = r_in[micro].astype(F32)
+        mean = jnp.mean(residual, axis=-1, keepdims=True)
+        centered = residual - mean
+        inverse = lax.rsqrt(jnp.mean(centered * centered, axis=-1, keepdims=True) + NORM_EPS)
+        stats[micro, :, 0:1] = mean
+        stats[micro, :, 1:2] = inverse
+        ops[0, micro] = (centered * inverse * gains[0, 0:1, :] + shifts[0, 0:1, :]).astype(BF16)
+        swap(0, 1, micro, 0).start()
 
         @pl.when(parity == 0)
         def _():
@@ -385,30 +385,30 @@
         def _():
             feed_forward(micro)
 
-        for half in (0, 1):
-            rows = halves[half]
-            unit, inverse = normalize(wide[rows])
-            units[micro, rows] = unit.astype(BF16)
-            inverses[micro, rows] = inverse
-
-            @pl.when(jnp.logical_not(last))
-            def _():
-                after = r_in[micro, rows].astype(F32) + unit * gains[0, 1:2, :] + shifts[0, 1:2, :]
-                r_out[micro, rows] = after.astype(BF16)
-                fwd_copy(micro, half).start()
+        unit, inverse = normalize(wide[...])
+
+        @pl.when(jnp.logical_not(last))
+        def _():
+            after = r_in[micro].astype(F32) + unit * gains[0, 1:2, :] + shifts[0, 1:2, :]
+            r_out[micro] = after.astype(BF16)
+            pl.when(micro > 0)(lambda: fwd_copy(micro - 1).wait_send())
+            fwd_copy(micro).start()
+
+        units[micro] = unit.astype(BF16)
+        stats[micro, :, 2:3] = inverse
+        pl.when(parity == 0)(lambda: swap(2, 1, micro, 0).start())
+        pl.when(parity == 1)(lambda: swap(2, 4, micro, 0).start())
 
     def backward(micro):
+        @pl.when(jnp.logical_not(last))
+        def _():
+            bwd_copy(micro).wait_recv()
+
         weight = sequence_weight(micro)
-        for half in (0, 1):
-            rows = halves[half]
-
-            @pl.when(jnp.logical_not(last))
-            def _():
-                bwd_copy(micro, half).wait_recv()
-
-            incoming = g_in[micro, rows].astype(F32) * weight
-            unit = units[micro, rows].astype(F32)
-            ops[1, micro, rows] = norm_backward(incoming, unit, inverses[micro, rows], gains[0, 1:2, :]).astype(BF16)
+        incoming = g_in[micro].astype(F32) * weight
+        unit = units[micro].astype(F32)
+        ops[1, micro] = norm_backward(incoming, unit, stats[micro, :, 2:3], gains[0, 1:2, :]).astype(BF16)
+        swap(1, 1, micro, 0).start()
 
         @pl.when(parity == 0)
         def _():
@@ -418,18 +418,15 @@
         def _():
             feed_backward(micro)
 
-        units_pre = []
-        for half in (0, 1):
-            rows = halves[half]
-            unit, inverse = normalize(r_in[micro, rows].astype(F32))
-            units_pre.append(unit)
-            incoming = g_in[micro, rows].astype(F32) * weight
-            grad = incoming + norm_backward(wide[rows], unit, inverse, gains[0, 0:1, :])
-            g_out[micro, rows] = grad.astype(BF16)
-
-            @pl.when(jnp.logical_not(first))
-            def _():
-                bwd_copy(micro, half).start()
+        inverse = stats[micro, :, 1:2]
+        unit = (r_in[micro].astype(F32) - stats[micro, :, 0:1]) * inverse
+        incoming = g_in[micro].astype(F32) * weight
+        grad = incoming + norm_backward(wide[...], unit, inverse, gains[0, 0:1, :])
+        g_out[micro] = grad.astype(BF16)
+
+        @pl.when(jnp.logical_not(first))
+        def _():
+            bwd_copy(micro).start()
 
         @pl.when(first)
         def _():
@@ -437,20 +434,32 @@
             for d in (1, 2, 3):
                 ig_copy(micro, d).start()
 
-        for half in (0, 1):
-            rows = halves[half]
-            incoming = g_in[micro, rows].astype(F32) * weight
-            small[0:1, :] += column_sum(wide[rows] * units_pre[half])
-            small[1:2, :] += column_sum(incoming * units[micro, rows].astype(F32))
-            small[2:3, :] += column_sum(wide[rows])
-            small[3:4, :] += column_sum(incoming)
-            small[4:5, :] += column_sum(ops[1, micro, rows].astype(F32))
+        r_out[micro] = wide[...].astype(BF16)
+        pl.when(parity == 0)(lambda: swap(6, 3, micro, 1).start())
+        pl.when(parity == 1)(lambda: swap(6, 4, micro, 1).start())
+
+    def row_sums(micro):
+        weight = sequence_weight(micro)
+        unit = (r_in[micro].astype(F32) - stats[micro, :, 0:1]) * stats[micro, :, 1:2]
+        grad = r_out[micro].astype(F32)
+        small[0:1, :] += column_sum(grad * unit)
+        small[2:3, :] += column_sum(grad)
+        incoming = g_in[micro].astype(F32) * weight
+        small[1:2, :] += column_sum(incoming * units[micro].astype(F32))
+        small[3:4, :] += column_sum(incoming)
+        small[4:5, :] += column_sum(ops[1, micro].astype(F32))
+        for j in range(4):
+            small[5 + j : 6 + j, :] += column_sum(ops[6 + j, micro].astype(F32))
 
     turn_at = jnp.where(section >= 2, 0, SLOTS)
 
     def step(t, carry):
         is_forward = jnp.where(last, (t + 1) % 2, jnp.where(t < SLOTS, 1, 0))
         micro = jnp.where(last, t // 2, t % SLOTS)
+
+        @pl.when((t == SLOTS) & jnp.logical_not(last))
+        def _():
+            fwd_copy(SLOTS - 1).wait_send()
 
         @pl.when(t == turn_at)
         def _():
@@ -477,7 +486,7 @@
         return device(section, x, (y + d) % 4, core)
 
     def chunk(q):
-        return jnp.where(parity == 1, q, jnp.where(q < 4, q + 4, q - 4))
+        return jnp.where(parity == 1, q, jnp.where(q < 4, 7 - q, q - 4))
 
     def at(q, h, b1, b2, n, c=None):
         c = core if c is None else c
@@ -499,29 +508,40 @@
     def arrived(like, sem):
         pltpu.make_async_copy(like, like, sem).wait()
 
-    def pair_copy(q):
-        rows = at(q, 0, 0, 0, 512, 1 - core)
-        return remote(buffer.at[rows], pair.at[q % 2], pair_send, pair_recv.at[q % 2], sibling)
+    def land_one(q, h, d):
+        return w1.at[pl.ds((q * 2 + h) * 64, 64), pl.ds(d * 512, 512)]
+
+    def land_two(q, h, d):
+        return w2t.at[pl.ds((q * 2 + h) * 64, 64), pl.ds(d * 1024, 1024)]
+
+    def land_three(q, h, d):
+        return w2t.at[pl.ds((q * 2 + h) * 64 + 16, 16), pl.ds(2048 + d * 1024, 512)]
+
+    def land_four(q, h, d):
+        return w2t.at[pl.ds((q * 2 + h) * 64, 16), pl.ds(2048 + d * 1024, 1024)]
+
+    def arrived_rows(rows, sem):
+        arrived(buffer.at[pl.ds(0, rows)], sem)
 
     def rs_one(q, h, d):
         p1, _ = spot(h)
         rows = at(q, h, (p1 + 2) % 4, 0, 64)
-        return ring(0, q, buffer.at[rows, left if d == 0 else right], r1.at[q, h, d], peer(h, 1 - 2 * d))
+        return ring(0, q, buffer.at[rows, left if d == 0 else right], land_one(q, h, d), peer(h, 1 - 2 * d))
 
     def rs_two(q, h, d):
         p1, _ = spot(h)
         step = 1 - 2 * d
-        return ring(1, q, buffer.at[at(q, h, (p1 + step) % 4, 0, 64)], r2.at[q, h, d], peer(h, step))
+        return ring(1, q, buffer.at[at(q, h, (p1 + step) % 4, 0, 64)], land_two(q, h, d), peer(h, step))
 
     def rs_three(q, h, d):
         p1, p2 = spot(h)
         rows = at(q, h, p1, (p2 + 2) % 4, 16)
-        return ring(2, q, buffer.at[rows, left if d == 0 else right], r3.at[q, h, d], peer(1 - h, 1 - 2 * d))
+        return ring(2, q, buffer.at[rows, left if d == 0 else right], land_three(q, h, d), peer(1 - h, 1 - 2 * d))
 
     def rs_four(q, h, d):
         p1, p2 = spot(h)
         step = 1 - 2 * d
-        return ring(3, q, buffer.at[at(q, h, p1, (p2 + step) % 4, 16)], r4.at[q, h, d], peer(1 - h, step))
+        return ring(3, q, buffer.at[at(q, h, p1, (p2 + step) % 4, 16)], land_four(q, h, d), peer(1 - h, step))
 
     def z_copy(k, h):
         p1, p2 = spot(h)
@@ -564,68 +584,65 @@
         piece = out_hbm.at[out_at(q, h, (p1 + d) % 4, 0, 64)]
         return remote(piece, piece, last_send, last_recv, sibling)
 
+    def swapped(group):
+        counts = ((3, 6), (3, 4))[group]
+        pl.when(parity == 0)(lambda: arrived_rows(counts[0] * ROWS, swap_recv.at[group]))
+        pl.when(parity == 1)(lambda: arrived_rows(counts[1] * ROWS, swap_recv.at[group]))
+
     def stage_0(q):
         k = chunk(q)
         feed_down = (parity == 1) & (k < 4)
         from_context = (parity == 0) & (k == 7)
         a = jnp.where(feed_down, 2 + k, jnp.where(from_context, 1, 0))
         b = jnp.where(feed_down, 1, jnp.where(from_context, 2, 2 + k))
-        right_side = ops[b].reshape(ROWS, WIDTH)
-        for cut in range(4):
-            left_side = ops[a, :, :, cut * 256 : (cut + 1) * 256].reshape(ROWS, 256)
-            product = dot_tn(left_side, right_side)
-            buffer[pl.ds(pl.multiple_of(k * 1024 + cut * 256, 256), 256), :] = product.astype(BF16)
-        pl.when(q >= 2)(lambda: pl.semaphore_wait(pair_free, 1))
-        pair_copy(q).start()
-
-    def stage_1(q):
-        pair_copy(q).wait_recv()
-        rows = at(q, 0, 0, 0, 512)
-        buffer[rows, :] = buffer[rows, :] + pair[q % 2]
-
-        @pl.when(q < 2 + 4 * parity)
-        def _():
-            pl.semaphore_signal(pair_free, inc=1, device_id=sibling, device_id_type=MESH)
-
+        pl.when(q == 0)(lambda: swapped(0))
+        pl.when(q == 1 + 3 * parity)(lambda: swapped(1))
+        right_own, right_other = ops[b].reshape(ROWS, WIDTH), other[b].reshape(ROWS, WIDTH)
+        for cut in range(2):
+            columns = pl.ds(pl.multiple_of(core * 512 + cut * 256, 256), 256)
+            product = dot_tn(ops[a, :, :, columns].reshape(ROWS, 256), right_own)
+            product = product + dot_tn(other[a, :, :, columns].reshape(ROWS, 256), right_other)
+            buffer[pl.ds(pl.multiple_of(k * 1024 + core * 512 + cut * 256, 256), 256), :] = product.astype(BF16)
+        pl.when(q == 0)(lambda: pl.semaphore_wait(ready, 4))
         for h, d in both:
             rs_one(q, h, d).start()
 
     def stage_2(q):
-        arrived(r1.at[q], ring_recv.at[0, q])
+        arrived_rows(128, ring_recv.at[0, q])
         for h, d in both:
             p1, _ = spot(h)
             rows = at(q, h, (p1 + 1 - 2 * d) % 4, 0, 64)
             cut = left if d == 0 else right
-            buffer[rows, cut] = buffer[rows, cut] + r1[q, h, d]
+            buffer[rows, cut] = buffer[rows, cut] + land_one(q, h, d)[...]
             rs_two(q, h, d).start()
 
     def stage_3(q):
-        arrived(r2.at[q], ring_recv.at[1, q])
+        arrived_rows(256, ring_recv.at[1, q])
         for h in (0, 1):
             p1, _ = spot(h)
             rows = at(q, h, p1, 0, 64)
-            total = buffer[rows, :].astype(F32) + r2[q, h, 0].astype(F32) + r2[q, h, 1].astype(F32)
+            total = buffer[rows, :].astype(F32) + land_two(q, h, 0)[...].astype(F32) + land_two(q, h, 1)[...].astype(F32)
             buffer[rows, :] = total.astype(BF16)
             for d in (0, 1):
                 rs_three(q, h, d).start()
 
     def stage_4(q):
-        arrived(r3.at[q], ring_recv.at[2, q])
+        arrived_rows(32, ring_recv.at[2, q])
         for h, d in both:
             p1, p2 = spot(h)
             rows = at(q, h, p1, (p2 + 1 - 2 * d) % 4, 16)
             cut = left if d == 0 else right
-            buffer[rows, cut] = buffer[rows, cut] + r3[q, h, d]
+            buffer[rows, cut] = buffer[rows, cut] + land_three(q, h, d)[...]
             rs_four(q, h, d).start()
 
     def stage_5(q):
         @pl.when((parity == 1) | (q < 4))
         def _():
-            arrived(r4.at[q], ring_recv.at[3, q])
+            arrived_rows(64, ring_recv.at[3, q])
             for h in (0, 1):
                 p1, p2 = spot(h)
                 rows = at(q, h, p1, p2, 16)
-                total = buffer[rows, :].astype(F32) + r4[q, h, 0].astype(F32) + r4[q, h, 1].astype(F32)
+                total = buffer[rows, :].astype(F32) + land_four(q, h, 0)[...].astype(F32) + land_four(q, h, 1)[...].astype(F32)
                 buffer[rows, :] = total.astype(BF16)
 
         @pl.when((parity == 1) & (q < 2))
@@ -648,20 +665,20 @@
                     ag_one(q, h, d).start()
 
     def stage_6(q):
-        arrived(r4.at[q], ring_recv.at[4, q])
+        arrived_rows(64, ring_recv.at[4, q])
         for h, d in both:
             ag_two(q, h, d).start()
-        arrived(r3.at[q], own_sem.at[q])
+        arrived_rows(32, own_sem.at[q])
 
     def stage_7(q):
-        arrived(r3.at[q], ring_recv.at[5, q])
+        arrived_rows(32, ring_recv.at[5, q])
         for h, d in both:
             ag_three(q, h, d).start()
         for h in (0, 1):
             last_copy(q, h, 0).start()
 
     def stage_8(q):
-        arrived(r2.at[q], ring_recv.at[6, q])
+        arrived_rows(256, ring_recv.at[6, q])
         for h, d in both:
             ag_four(q, h, d).start()
         for h in (0, 1):
@@ -669,11 +686,11 @@
             last_copy(q, h, 3).start()
 
     def stage_9(q):
-        arrived(r1.at[q], ring_recv.at[7, q])
+        arrived_rows(128, ring_recv.at[7, q])
         for h in (0, 1):
             last_copy(q, h, 2).start()
 
-    stages = [stage_0, stage_1, stage_2, stage_3, stage_4, stage_5, stage_6, stage_7, stage_8, stage_9]
+    stages = [stage_0, None, stage_2, stage_3, stage_4, stage_5, stage_6, stage_7, stage_8, stage_9]
 
     def tiny(phase, d):
         if phase == 0:
@@ -717,9 +734,14 @@
         for d in (1, 2, 3):
             tiny(3, d).start()
 
+    for axis in (0, 1):
+        for d in (1, 3):
+            pl.semaphore_signal(ready, inc=1, device_id=peer(axis, d), device_id_type=MESH)
+
     def slot(t, carry):
+        pl.when((t >= 3) & (t < 3 + SLOTS))(lambda: row_sums(t - 3))
         for number, turn in enumerate((tiny_0, tiny_1, tiny_2, tiny_3)):
-            pl.when(t == number)(turn)
+            pl.when(t == 3 + SLOTS + number)(turn)
         for s in ORDER:
             k = t - jnp.where(parity == 1, OFFSET_FEED[s], OFFSET_ATTEND[s])
             live = (k >= 0) & (k < CHUNKS)
@@ -744,30 +766,23 @@
 
     @pl.when(parity == 1)
     def _():
-        sent(8 * 512, pair_send)
+        sent(10 * ROWS, swap_send)
         sent(8 * 480, ring_send.at[0])
         sent(2 * 32, z_send)
 
     @pl.when(parity == 0)
     def _():
-        sent(4 * 512, pair_send)
+        sent(6 * ROWS, swap_send)
         sent(4 * 480, ring_send.at[0])
 
     sent(6 * 480, ring_send.at[1])
     sent(6 * 512, last_send)
     sent(6 * 512, last_recv)
 
-    @pl.when(jnp.logical_not(last))
+    @pl.when(jnp.logical_not(first))
     def _():
         for micro in range(SLOTS):
-            for half in (0, 1):
-                fwd_copy(micro, half).wait_send()
-
-    @pl.when(jnp.logical_not(first))
-    def _():
-        for micro in range(SLOTS):
-            for half in (0, 1):
-                bwd_copy(micro, half).wait_send()
+            bwd_copy(micro).wait_send()
             ig_copy(micro, 1).wait_recv()
 
     @pl.when(first)
@@ -804,8 +819,9 @@
             pltpu.VMEM((2 * FF, WIDTH), BF16),
             pltpu.VMEM((WIDTH, FF), BF16),
             pltpu.VMEM((10, SLOTS, LEN, WIDTH), BF16),
+            pltpu.VMEM((10, SLOTS, LEN, WIDTH), BF16),
             pltpu.VMEM((SLOTS, LEN, WIDTH), BF16),
-            pltpu.VMEM((SLOTS, LEN, 1), F32),
+            pltpu.VMEM((SLOTS, LEN, 3), F32),
             pltpu.VMEM((SLOTS, LEN, WIDTH), BF16),
             pltpu.VMEM((SLOTS, LEN, WIDTH), BF16),
             pltpu.VMEM((SLOTS, LEN, WIDTH), BF16),
@@ -813,18 +829,13 @@
             pltpu.VMEM((LEN, WIDTH), F32),
             pltpu.VMEM((16, WIDTH), F32),
             pltpu.VMEM((16, WIDTH), F32),
-            pltpu.VMEM((2, 512, WIDTH), BF16),
-            pltpu.VMEM((CHUNKS, 2, 2, 64, 512), BF16),
-            pltpu.VMEM((CHUNKS, 2, 2, 64, WIDTH), BF16),
-            pltpu.VMEM((CHUNKS, 2, 2, 16, 512), BF16),
-            pltpu.VMEM((CHUNKS, 2, 2, 16, WIDTH), BF16),
             pltpu.VMEM((2, 2, 16, WIDTH), BF16),
             pltpu.VMEM((3, 16, WIDTH), F32),
             pltpu.VMEM((3, 16, WIDTH), F32),
             pltpu.VMEM((16, WIDTH), F32),
             pltpu.VMEM((3, 16, WIDTH), F32),
             dma((12,)), dma((2,)), dma((2,)), dma((20,)), dma((20,)),
-            dma((SLOTS, 2)), dma((SLOTS, 2)), dma((SLOTS, 2)), dma((SLOTS, 2)),
+            dma((SLOTS,)), dma((SLOTS,)), dma((SLOTS,)), dma((SLOTS,)),
             dma((SLOTS, 4)), dma((SLOTS,)),
             dma, dma((2,)), pltpu.SemaphoreType.REGULAR,
             dma((2,)), dma((8, CHUNKS)), dma, dma((2, 2)), dma((CHUNKS,)), dma, dma,

time: 206 us -> 198 us (0.961)
  Pallas kernels: 204 us -> 197 us
    pallas_call x1, Pallas kernels: 192 us -> 184 us  [mega(): pl.pallas_call(mega_kernel, name='mega', out_shape=[jax.ShapeDtypeStruct(...]
where the time goes in v3:
time: 198 us
  Pallas kernels  197 us (99%)
    pallas_call x1, Pallas kernels, mega(): pl.pallas_call(mega_kernel, name='mega', out_shape=[jax.ShapeDtypeStruct(...  184 us
    pallas_call x1, Pallas kernels, widen(): pl.pallas_call(widen_kernel, name='widen', out_shape=[jax.ShapeDtypeStruc...  12.4 us

profile of v3, /device:TPU:33, one launch (start us, length us, event | category | flops | bytes accessed | tf_op | source)
XLA Modules:
  0.0 198.0 jit_solution(6366881397607617955)
XLA Ops:
  1.3 184.2 %mega.1 = (bf16[6144,1024]{1,0:T(8,128)(2,1)}, f32[5,16,1024]{2,1,0:T(8,128)}, bf16[4,128,256]{2,1,0:T(8,128)(2,1)}) custom-call(bf16[4,128,1024]{2,1,0:T(8,128)(2,1)} %block_hbm.1, bf16[4,128,1024]{2,1,0:T(8,128)(2,1)} %cot_hbm.1, s32[4]{0:T(128)} %group_hbm.1, s32[1]{0:T(128)S(6)} %copy.20.live_hbm, f32[8]{0:T(128)} %scale_hbm.1, f32[1,2,1024]{2,1,0:T(2,128)} %gains_hbm.1, ...), custom_call_target="tpu_custom_call" | custom-call | tf_op jit(solution)/shard_map/mega/pallas_call | solution.py:799
  185.4 12.4 %widen.1 = (f32[1,1024,4096]{2,1,0:T(8,128)}, f32[2048,1024]{1,0:T(8,128)}, f32[2,2,1024]{2,1,0:T(2,128)}, f32[2,4096]{1,0:T(2,128)}, f32[1,1024]{1,0:T(1,128)},...) custom-call(bf16[6144,1024]{1,0:T(8,128)(2,1)} %get-tuple-element.19.reduced, ...), custom_call_target="tpu_custom_call" | custom-call | tf_op jit(solution)/shard_map/widen/pallas_call | solution.py:909

commit v4 on v3

--- a/solution.py
+++ b/solution.py
@@ -21,9 +21,9 @@
 NORM_EPS = 1e-05
 GELU_C = math.sqrt(2.0 / math.pi)
 CHUNKS = 8
-ORDER = (0, 3, 4, 5, 8, 9, 6, 7, 2)
-OFFSET_FEED = (0, 0, 1, 3, 4, 5, 6, 7, 10, 12)
-OFFSET_ATTEND = (0, 0, 4, 6, 7, 8, 9, 10, 13, 15)
+ORDER = (7, 0, 3, 8, 4, 5, 6, 2, 9)
+OFFSET_FEED = (0, 0, 1, 3, 4, 5, 6, 8, 10, 12)
+OFFSET_ATTEND = (0, 0, 1, 3, 4, 5, 6, 8, 11, 14)
 
 
 def device(section, x, y, core):
@@ -101,7 +101,7 @@
     z, sx, sy, ss, sums,
     load_sem, down_send, down_recv, ag_send, ag_recv,
     fwd_send, fwd_recv, bwd_send, bwd_recv, ig_send, ig_recv,
-    swap_send, swap_recv, ready, ring_send, ring_recv, z_send, z_recv, own_sem, last_send, last_recv,
+    swap_send, swap_recv, ready, ring_send, ring_recv, z_send, z_recv, export_send, export_recv, own_sem, last_send, last_recv,
     tiny_send, tiny_recv,
 ):
     section, x, y, core = place()
@@ -141,38 +141,54 @@
 
     greet(section, x, y, core)
 
-    row_a = core * 512 + y * 128 + x * 32
-    row_b = 1024 + core * 512 + x * 128 + y * 32
-
-    def down_copy(half):
-        row = row_a if half == 0 else row_b
+    left, right = pl.ds(0, 512), pl.ds(512, 512)
+    both = [(h, d) for h in (0, 1) for d in (0, 1)]
+
+    def peer(axis, d):
+        if axis == 0:
+            return device(section, (x + d) % 4, y, core)
+        return device(section, x, (y + d) % 4, core)
+
+    def arrived_rows(rows, sem):
+        piece = buffer.at[pl.ds(0, rows)]
+        pltpu.make_async_copy(piece, piece, sem).wait()
+
+    def down_rows(h, p, major, minor, n):
+        row = h * 1024 + core * 512 + p * 256 + major * 64 + minor * 16
+        return pl.ds(pl.multiple_of(row, 16), n)
+
+    def down_spot(h):
+        return (y, x) if h == 0 else (x, y)
+
+    def down_copy(p, h):
+        rows = down_rows(h, p, *down_spot(h), 16)
         return remote(
-            down_hbm.at[pl.ds(row, 32)], w2.at[pl.ds(row, 32)], down_send.at[half], down_recv.at[half],
-            device((section + 1) % 4, x, y, core),
+            down_hbm.at[rows], w2.at[rows], down_send, down_recv.at[p], device((section + 1) % 4, x, y, core)
         )
 
-    def ag_copy(index):
-        d = index % 3 + 1
-        along_x = device(section, (x + d) % 4, y, core)
-        along_y = device(section, x, (y + d) % 4, core)
-        if index < 3:
-            rows, to = pl.ds(row_a, 32), along_x
-        elif index < 6:
-            rows, to = pl.ds(row_b, 32), along_y
-        elif index < 9:
-            rows, to = pl.ds(core * 512 + y * 128, 128), along_y
-        elif index < 12:
-            rows, to = pl.ds(1024 + core * 512 + x * 128, 128), along_x
-        elif index < 16:
-            rows, to = pl.ds(core * 512 + (y + index - 12) % 4 * 128, 128), sibling
-        else:
-            rows, to = pl.ds(1024 + core * 512 + (x + index - 16) % 4 * 128, 128), sibling
-        return remote(w2.at[rows], w2.at[rows], ag_send.at[index], ag_recv.at[index], to)
+    def down_near(p, h, d):
+        rows = down_rows(h, p, *down_spot(h), 16)
+        return remote(w2.at[rows], w2.at[rows], ag_send, ag_recv.at[0, p], peer(h, d))
+
+    def down_ring(p, h, d):
+        rows = down_rows(h, p, down_spot(h)[0], 0, 64)
+        return remote(w2.at[rows], w2.at[rows], ag_send, ag_recv.at[1, p], peer(1 - h, 1 - 2 * d))
+
+    def down_pass(p, h, d):
+        step = 1 - 2 * d
+        rows = down_rows(h, p, (down_spot(h)[0] - step) % 4, 0, 64)
+        piece = w2.at[rows, left if d == 0 else right]
+        return remote(piece, piece, ag_send, ag_recv.at[2, p], peer(1 - h, step))
+
+    def down_share(p, h, d):
+        rows = down_rows(h, p, (down_spot(h)[0] + d) % 4, 0, 64)
+        return remote(w2.at[rows], w2.at[rows], ag_send, ag_recv.at[3, 0], sibling)
 
     @pl.when(parity == 0)
     def _():
-        down_copy(0).start()
-        down_copy(1).start()
+        for p in (0, 1):
+            for h in (0, 1):
+                down_copy(p, h).start()
 
     for copy in load_pieces:
         copy.wait()
@@ -199,33 +215,38 @@
     small[...] = jnp.zeros_like(small)
 
     def gather_start():
-        for half in (0, 1):
-            down_copy(half).wait_recv()
-            for index in range(3 * half, 3 * half + 3):
-                ag_copy(index).start()
-        for half in (0, 1):
-            for index in range(3 * half, 3 * half + 3):
-                ag_copy(index).wait()
-            for index in range(6 + 3 * half, 9 + 3 * half):
-                ag_copy(index).start()
-            ag_copy(12 + 4 * half).start()
+        for p in (0, 1):
+            arrived_rows(32, down_recv.at[p])
+            for h in (0, 1):
+                for d in (1, 3, 2):
+                    down_near(p, h, d).start()
+        for p in (0, 1):
+            arrived_rows(96, ag_recv.at[0, p])
+            for h, d in both:
+                down_ring(p, h, d).start()
+            for h in (0, 1):
+                down_share(p, h, 0).start()
+        gather_pass(0)
         load_own.wait()
 
+    def gather_pass(p):
+        arrived_rows(256, ag_recv.at[1, p])
+        for h, d in both:
+            down_pass(p, h, d).start()
+        for h in (0, 1):
+            down_share(p, h, 1).start()
+            down_share(p, h, 3).start()
+
     def gather_end():
-        for d in (1, 3, 2):
-            for half in (0, 1):
-                ag_copy(5 + 3 * half + 4 - d).wait()
-                ag_copy(12 + 4 * half + d).start()
-        for index in range(12, 20):
-            ag_copy(index).wait()
+        gather_pass(1)
+        for p in (0, 1):
+            arrived_rows(128, ag_recv.at[2, p])
+            for h in (0, 1):
+                down_share(p, h, 2).start()
+        arrived_rows(1024, ag_recv.at[3, 0])
 
     pl.when(parity == 1)(gather_start)
     pl.when(last)(gather_end)
-
-    @pl.when(parity == 0)
-    def _():
-        down_copy(0).wait_send()
-        down_copy(1).wait_send()
 
     load_w1.wait()
 
@@ -480,18 +501,44 @@
     def spot(h):
         return (x, y) if h == 0 else (y, x)
 
-    def peer(axis, d):
-        if axis == 0:
-            return device(section, (x + d) % 4, y, core)
-        return device(section, x, (y + d) % 4, core)
+    sends_out = section == 1
+    takes_in = section == 2
 
     def chunk(q):
-        return jnp.where(parity == 1, q, jnp.where(q < 4, 7 - q, q - 4))
-
-    def at(q, h, b1, b2, n, c=None):
-        c = core if c is None else c
-        row = chunk(q) * 1024 + c * 512 + h * 256 + b1 * 64 + b2 * 16
+        late = jnp.where(takes_in, jnp.where(q == 7, 2, q - 4), jnp.where(q == 4, 1, 0))
+        return jnp.where(parity == 1, q, jnp.where(q < 4, 7 - q, late))
+
+    def exported(q):
+        return sends_out & (q == 0)
+
+    def imported(q):
+        return takes_in & (q == 7)
+
+    def multiplies(q):
+        return (parity == 1) | (q < 4)
+
+    def reduces(q):
+        return (multiplies(q) & jnp.logical_not(exported(q))) | imported(q)
+
+    def hands_over(q):
+        return ((section == 3) & (q < 2)) | (sends_out & (q == 1)) | imported(q)
+
+    def takes_over(q):
+        return ((section == 0) & ((q == 4) | (q == 6))) | (takes_in & ((q == 4) | (q == 5)))
+
+    def gathers(q):
+        return ((parity == 1) & (q >= 2)) | ((parity == 0) & (q < 4)) | takes_over(q)
+
+    def at(q, h, b1, b2, n):
+        row = chunk(q) * 1024 + core * 512 + h * 256 + b1 * 64 + b2 * 16
         return pl.ds(pl.multiple_of(row, 16), n)
+
+    def export_copy():
+        return remote(
+            buffer.at[pl.ds(pl.multiple_of(core * 512, 512), 512)],
+            buffer.at[pl.ds(pl.multiple_of(2048 + core * 512, 512), 512)],
+            export_send, export_recv, device((section + 1) % 4, x, y, core),
+        )
 
     def out_at(q, h, b1, b2, n):
         k = chunk(q)
@@ -499,15 +546,9 @@
         row = k * 1024 + core * 512 + h * 256 + b1 * 64 + b2 * 16
         return pl.ds(pl.multiple_of(row, 16), n)
 
-    left, right = pl.ds(0, 512), pl.ds(512, 512)
-    both = [(h, d) for h in (0, 1) for d in (0, 1)]
-
     def ring(stage, q, source, target, to):
         return remote(source, target, ring_send.at[stage // 4], ring_recv.at[stage, q], to)
 
-    def arrived(like, sem):
-        pltpu.make_async_copy(like, like, sem).wait()
-
     def land_one(q, h, d):
         return w1.at[pl.ds((q * 2 + h) * 64, 64), pl.ds(d * 512, 512)]
 
@@ -519,9 +560,6 @@
 
     def land_four(q, h, d):
         return w2t.at[pl.ds((q * 2 + h) * 64, 16), pl.ds(2048 + d * 1024, 1024)]
-
-    def arrived_rows(rows, sem):
-        arrived(buffer.at[pl.ds(0, rows)], sem)
 
     def rs_one(q, h, d):
         p1, _ = spot(h)
@@ -543,13 +581,16 @@
         step = 1 - 2 * d
         return ring(3, q, buffer.at[at(q, h, p1, (p2 + step) % 4, 16)], land_four(q, h, d), peer(1 - h, step))
 
-    def z_copy(k, h):
+    def z_copy(q, h):
         p1, p2 = spot(h)
-        row = k * 1024 + core * 512 + h * 256 + p1 * 64 + p2 * 16
+        to = jnp.where(takes_in, 0, section - 1)
+        slot = jnp.where(takes_in, 0, chunk(q))
         return remote(
-            buffer.at[pl.ds(pl.multiple_of(row, 16), 16)], z.at[k, h], z_send, z_recv.at[k, h],
-            device((section + 3) % 4, x, y, core),
+            buffer.at[at(q, h, p1, p2, 16)], z.at[slot, h], z_send, z_recv.at[slot, h], device(to, x, y, core)
         )
+
+    def z_arrival(q, h):
+        return remote(z.at[chunk(q), h], z.at[chunk(q), h], z_send, z_recv.at[chunk(q), h], sibling)
 
     def own_copy(q, h):
         p1, p2 = spot(h)
@@ -589,7 +630,7 @@
         pl.when(parity == 0)(lambda: arrived_rows(counts[0] * ROWS, swap_recv.at[group]))
         pl.when(parity == 1)(lambda: arrived_rows(counts[1] * ROWS, swap_recv.at[group]))
 
-    def stage_0(q):
+    def multiply(q):
         k = chunk(q)
         feed_down = (parity == 1) & (k < 4)
         from_context = (parity == 0) & (k == 7)
@@ -603,9 +644,17 @@
             product = dot_tn(ops[a, :, :, columns].reshape(ROWS, 256), right_own)
             product = product + dot_tn(other[a, :, :, columns].reshape(ROWS, 256), right_other)
             buffer[pl.ds(pl.multiple_of(k * 1024 + core * 512 + cut * 256, 256), 256), :] = product.astype(BF16)
-        pl.when(q == 0)(lambda: pl.semaphore_wait(ready, 4))
-        for h, d in both:
-            rs_one(q, h, d).start()
+
+    def stage_0(q):
+        pl.when(multiplies(q))(lambda: multiply(q))
+        pl.when(exported(q))(lambda: export_copy().start())
+        pl.when(imported(q))(lambda: export_copy().wait_recv())
+
+        @pl.when(reduces(q))
+        def _():
+            pl.when(q == jnp.where(sends_out, 1, 0))(lambda: pl.semaphore_wait(ready, 4))
+            for h, d in both:
+                rs_one(q, h, d).start()
 
     def stage_2(q):
         arrived_rows(128, ring_recv.at[0, q])
@@ -636,28 +685,28 @@
             rs_four(q, h, d).start()
 
     def stage_5(q):
-        @pl.when((parity == 1) | (q < 4))
+        @pl.when(reduces(q))
         def _():
             arrived_rows(64, ring_recv.at[3, q])
             for h in (0, 1):
                 p1, p2 = spot(h)
                 rows = at(q, h, p1, p2, 16)
-                total = buffer[rows, :].astype(F32) + land_four(q, h, 0)[...].astype(F32) + land_four(q, h, 1)[...].astype(F32)
-                buffer[rows, :] = total.astype(BF16)
-
-        @pl.when((parity == 1) & (q < 2))
+                arrival = land_four(q, h, 0)[...].astype(F32) + land_four(q, h, 1)[...].astype(F32)
+                buffer[rows, :] = (buffer[rows, :].astype(F32) + arrival).astype(BF16)
+
+        @pl.when(hands_over(q))
         def _():
             for h in (0, 1):
                 z_copy(q, h).start()
 
-        @pl.when((parity == 0) & (q >= 4))
+        @pl.when(takes_over(q))
         def _():
             for h in (0, 1):
                 p1, p2 = spot(h)
-                z_copy(q - 4, h).wait_recv()
-                buffer[at(q, h, p1, p2, 16), :] = z[q - 4, h]
-
-        @pl.when((parity == 0) | (q >= 2))
+                z_arrival(q, h).wait_recv()
+                buffer[at(q, h, p1, p2, 16), :] = z[chunk(q), h]
+
+        @pl.when(gathers(q))
         def _():
             for h in (0, 1):
                 own_copy(q, h).start()
@@ -734,6 +783,7 @@
         for d in (1, 2, 3):
             tiny(3, d).start()
 
+    pl.when(parity == 1)(lambda: arrived_rows(1984, ag_send))
     for axis in (0, 1):
         for d in (1, 3):
             pl.semaphore_signal(ready, inc=1, device_id=peer(axis, d), device_id_type=MESH)
@@ -745,12 +795,14 @@
         for s in ORDER:
             k = t - jnp.where(parity == 1, OFFSET_FEED[s], OFFSET_ATTEND[s])
             live = (k >= 0) & (k < CHUNKS)
-            if s < 5:
-                live = live & ((parity == 1) | (k < 4))
+            if s == 0:
+                live = live & (multiplies(k) | imported(k))
+            elif s < 5:
+                live = live & reduces(k)
             elif s == 5:
-                live = live & ((parity == 1) | (k < 6))
+                live = live & (reduces(k) | gathers(k))
             else:
-                live = live & jnp.where(parity == 1, k >= 2, k < 6)
+                live = live & gathers(k)
             pl.when(live)(lambda turn=stages[s], k=k: turn(k))
         return carry
 
@@ -762,19 +814,19 @@
         copy.wait()
 
     def sent(rows, sem):
-        arrived(buffer.at[pl.ds(0, rows)], sem)
-
-    @pl.when(parity == 1)
-    def _():
-        sent(10 * ROWS, swap_send)
-        sent(8 * 480, ring_send.at[0])
-        sent(2 * 32, z_send)
-
-    @pl.when(parity == 0)
-    def _():
-        sent(6 * ROWS, swap_send)
-        sent(4 * 480, ring_send.at[0])
-
+        arrived_rows(rows, sem)
+
+    pl.when(parity == 1)(lambda: sent(10 * ROWS, swap_send))
+    pl.when(parity == 0)(lambda: sent(6 * ROWS, swap_send))
+    pl.when(parity == 0)(lambda: sent(64, down_send))
+    for number, (ring_count, z_count) in enumerate(((4, 0), (7, 1), (5, 1), (8, 2))):
+        @pl.when(section == number)
+        def _():
+            sent(ring_count * 480, ring_send.at[0])
+            if z_count:
+                sent(z_count * 32, z_send)
+
+    pl.when(sends_out)(lambda: export_copy().wait_send())
     sent(6 * 480, ring_send.at[1])
     sent(6 * 512, last_send)
     sent(6 * 512, last_recv)
@@ -834,11 +886,11 @@
             pltpu.VMEM((3, 16, WIDTH), F32),
             pltpu.VMEM((16, WIDTH), F32),
             pltpu.VMEM((3, 16, WIDTH), F32),
-            dma((12,)), dma((2,)), dma((2,)), dma((20,)), dma((20,)),
+            dma((12,)), dma, dma((2,)), dma, dma((4, 2)),
             dma((SLOTS,)), dma((SLOTS,)), dma((SLOTS,)), dma((SLOTS,)),
             dma((SLOTS, 4)), dma((SLOTS,)),
             dma, dma((2,)), pltpu.SemaphoreType.REGULAR,
-            dma((2,)), dma((8, CHUNKS)), dma, dma((2, 2)), dma((CHUNKS,)), dma, dma,
+            dma((2,)), dma((8, CHUNKS)), dma, dma((2, 2)), dma, dma, dma((CHUNKS,)), dma, dma,
             dma((12,)), dma((12,)),
         ],
         compiler_params=pltpu.CompilerParams(

time: 198 us -> 195 us (0.985)
  Pallas kernels: 197 us -> 192 us
    pallas_call x1, Pallas kernels: 184 us -> 180 us  [mega(): pl.pallas_call(mega_kernel, name='mega', out_shape=[jax.ShapeDtypeStruct(...]
where the time goes in v4:
time: 195 us; the launch traced here: 193 us
  Pallas kernels  192 us (98%)
    pallas_call x1, Pallas kernels, mega(): pl.pallas_call(mega_kernel, name='mega', out_shape=[jax.ShapeDtypeStruct(...  180 us
    pallas_call x1, Pallas kernels, widen(): pl.pallas_call(widen_kernel, name='widen', out_shape=[jax.ShapeDtypeStruc...  12.4 us

profile of v4, /device:TPU:33, one launch (start us, length us, event | category | flops | bytes accessed | tf_op | source)
XLA Modules:
  0.0 193.3 jit_solution(3320779824502330047)
XLA Ops:
  1.3 179.5 %mega.1 = (bf16[6144,1024]{1,0:T(8,128)(2,1)}, f32[5,16,1024]{2,1,0:T(8,128)}, bf16[4,128,256]{2,1,0:T(8,128)(2,1)}) custom-call(bf16[4,128,1024]{2,1,0:T(8,128)(2,1)} %block_hbm.1, bf16[4,128,1024]{2,1,0:T(8,128)(2,1)} %cot_hbm.1, s32[4]{0:T(128)} %group_hbm.1, s32[1]{0:T(128)S(6)} %copy.20.live_hbm, f32[8]{0:T(128)} %scale_hbm.1, f32[1,2,1024]{2,1,0:T(2,128)} %gains_hbm.1, ...), custom_call_target="tpu_custom_call" | custom-call | tf_op jit(solution)/shard_map/mega/pallas_call | solution.py:851
  180.8 12.4 %widen.1 = (f32[1,1024,4096]{2,1,0:T(8,128)}, f32[2048,1024]{1,0:T(8,128)}, f32[2,2,1024]{2,1,0:T(2,128)}, f32[2,4096]{1,0:T(2,128)}, f32[1,1024]{1,0:T(1,128)},...) custom-call(bf16[6144,1024]{1,0:T(8,128)(2,1)} %get-tuple-element.19.reduced, ...), custom_call_target="tpu_custom_call" | custom-call | tf_op jit(solution)/shard_map/widen/pallas_call | solution.py:961

commit v5 on v4

--- a/solution.py
+++ b/solution.py
@@ -100,7 +100,7 @@
     w1, buffer, w2t, ops, other, units, stats, r_in, r_out, g_in, g_out, wide, small, vectors,
     z, sx, sy, ss, sums,
     load_sem, down_send, down_recv, ag_send, ag_recv,
-    fwd_send, fwd_recv, bwd_send, bwd_recv, ig_send, ig_recv,
+    fwd_send, fwd_recv, bwd_send, bwd_recv, ig_send, ig_recv, token,
     swap_send, swap_recv, ready, ring_send, ring_recv, z_send, z_recv, export_send, export_recv, own_sem, last_send, last_recv,
     tiny_send, tiny_recv,
 ):
@@ -227,6 +227,7 @@
             for h in (0, 1):
                 down_share(p, h, 0).start()
         gather_pass(0)
+        gather_pass(1)
         load_own.wait()
 
     def gather_pass(p):
@@ -238,7 +239,6 @@
             down_share(p, h, 3).start()
 
     def gather_end():
-        gather_pass(1)
         for p in (0, 1):
             arrived_rows(128, ag_recv.at[2, p])
             for h in (0, 1):
@@ -309,35 +309,46 @@
         for j in range(3):
             part = dot(normed, w1[:, j * WIDTH : (j + 1) * WIDTH]) + vectors[5 + j : 6 + j, :]
             ops[6 + j, micro] = part.astype(BF16)
-        rows = lax.broadcasted_iota(jnp.int32, (LEN, 256), 0)
-        columns = lax.broadcasted_iota(jnp.int32, (LEN, 256), 1) % 128
-        causal = rows >= columns
+        rows = lax.broadcasted_iota(jnp.int32, (LEN, LEN), 0)
+        columns = lax.broadcasted_iota(jnp.int32, (LEN, LEN), 1)
+        causal = rows <= columns
         for p in range(PAIRS):
             cut = slice(p * 128, (p + 1) * 128)
             query, key, value = (ops[6 + j, micro, :, cut] for j in range(3))
-            scores = dot_nt(query, two_heads(key)) * 0.125
-            scores = jnp.where(causal, scores, -1e9)
-            halves = []
-            for half in (scores[:, :128], scores[:, 128:]):
-                powers = jnp.exp(half - jnp.max(half, axis=-1, keepdims=True))
-                halves.append((powers / jnp.sum(powers, axis=-1, keepdims=True)).astype(BF16))
-            weights = jnp.concatenate(halves, axis=1)
-            ops[3 + p // 4, micro, :, (p % 4) * 256 : (p % 4 + 1) * 256] = weights
-            ops[2, micro, :, cut] = dot(weights, two_heads(value)).astype(BF16)
+            scores = dot_nt(two_heads(key), query) * 0.125
+            parts = []
+            for head in (0, 1):
+                part = jnp.where(causal, scores[head * LEN : (head + 1) * LEN], -1e9)
+                powers = jnp.exp(part - jnp.max(part, axis=0, keepdims=True))
+                part = (powers / jnp.sum(powers, axis=0, keepdims=True)).astype(BF16)
+                ops[3 + p // 4, micro, :, (p % 4 * 2 + head) * 128 : (p % 4 * 2 + head + 1) * 128] = part
+                parts.append(part)
+            ops[2, micro, :, cut] = dot_tn(jnp.concatenate(parts, axis=0), two_heads(value)).astype(BF16)
         wide[...] = dot_nt(ops[2, micro], w1[:, 3 * WIDTH :]) + out_bias[...]
 
     def feed_forward(micro):
         normed = ops[0, micro]
         branch = out_bias[...]
-        for j in (2, 3, 0, 1):
-            hidden = dot(normed, w1[:, j * WIDTH : (j + 1) * WIDTH]) + vectors[5 + j : 6 + j, :]
+        def product(j):
+            b, cut = j * 256 // WIDTH, slice(j * 256 % WIDTH, j * 256 % WIDTH + 256)
+            return dot(normed, w1[:, j * 256 : (j + 1) * 256]) + vectors[5 + b : 6 + b, cut]
+
+        def gate(j, hidden):
+            b, cut = j * 256 // WIDTH, slice(j * 256 % WIDTH, j * 256 % WIDTH + 256)
             square = hidden * hidden
-            along = jnp.tanh(hidden * (GELU_C + (GELU_C * 0.044715) * square))
-            above = 0.5 * (1.0 + along)
-            slope = above + 0.5 * hidden * (1.0 - along * along) * (GELU_C + (3.0 * GELU_C * 0.044715) * square)
-            active = (hidden * above).astype(BF16)
-            ops[6 + j, micro] = slope.astype(BF16)
-            ops[2 + j, micro] = active
+            above = 0.5 + 0.5 * jnp.tanh(hidden * (GELU_C + (GELU_C * 0.044715) * square))
+            active = hidden * above
+            slope = above + (active - active * above) * (2.0 * GELU_C + (6.0 * GELU_C * 0.044715) * square)
+            ops[6 + b, micro, :, cut] = slope.astype(BF16)
+            ops[2 + b, micro, :, cut] = active.astype(BF16)
+
+        order = (8, 9, 10, 11, 12, 13, 14, 15, 0, 1, 2, 3, 4, 5, 6, 7)
+        hidden = product(order[0])
+        for step, j in enumerate(order):
+            ahead = product(order[step + 1]) if step + 1 < len(order) else None
+            gate(j, hidden)
+            hidden = ahead
+        branch = out_bias[...]
         for j in (2, 3, 0, 1):
             if j == 0:
                 pl.when((micro == 0) & (section == 1))(gather_end)
@@ -350,18 +361,19 @@
             cut = slice(p * 128, (p + 1) * 128)
             query, key, value = (ops[6 + j, micro, :, cut] for j in range(3))
             grad = ops[9, micro, :, cut]
-            weights = ops[3 + p // 4, micro, :, (p % 4) * 256 : (p % 4 + 1) * 256]
-            grad_weights = dot_nt(grad, two_heads(value))
-            weights_wide = weights.astype(F32)
-            product = weights_wide * grad_weights
-            left = product[:, :128] - weights_wide[:, :128] * jnp.sum(product[:, :128], axis=-1, keepdims=True)
-            right = product[:, 128:] - weights_wide[:, 128:] * jnp.sum(product[:, 128:], axis=-1, keepdims=True)
-            grad_scores = jnp.concatenate([left, right], axis=1).astype(BF16)
-            grad_query = dot(grad_scores, two_heads(key)) * 0.125
-            both = dot_tn(grad_scores, query) * 0.125
-            grad_key = jnp.where(low_lanes, both[:128], both[128:])
-            both = dot_tn(weights, grad)
-            grad_value = jnp.where(low_lanes, both[:128], both[128:])
+            parts = [ops[3 + p // 4, micro, :, (p % 4 * 2 + h) * 128 : (p % 4 * 2 + h + 1) * 128] for h in (0, 1)]
+            grad_weights = dot_nt(two_heads(value), grad)
+            grad_scores = []
+            for head in (0, 1):
+                part = parts[head].astype(F32)
+                product = part * grad_weights[head * LEN : (head + 1) * LEN]
+                grad_scores.append((product - part * jnp.sum(product, axis=0, keepdims=True)).astype(BF16))
+            grad_scores = jnp.concatenate(grad_scores, axis=0)
+            grad_query = dot_tn(grad_scores, two_heads(key)) * 0.125
+            both_heads = dot(grad_scores, query) * 0.125
+            grad_key = jnp.where(low_lanes, both_heads[:LEN], both_heads[LEN:])
+            both_heads = dot(jnp.concatenate(parts, axis=0), grad)
+            grad_value = jnp.where(low_lanes, both_heads[:LEN], both_heads[LEN:])
             for j, part in enumerate((grad_query, grad_key, grad_value)):
                 ops[6 + j, micro, :, cut] = part.astype(BF16)
         total = jnp.zeros((LEN, WIDTH), F32)
@@ -412,8 +424,16 @@
         def _():
             after = r_in[micro].astype(F32) + unit * gains[0, 1:2, :] + shifts[0, 1:2, :]
             r_out[micro] = after.astype(BF16)
-            pl.when(micro > 0)(lambda: fwd_copy(micro - 1).wait_send())
+            leads = (section == 1) & (core == 1)
+            follows = (section == 1) & (core == 0)
+            pl.when(micro > jnp.where(leads, 1, 0))(lambda: fwd_copy(micro - 1).wait_send())
+            pl.when(follows & (micro == 0))(lambda: pl.semaphore_wait(token, 1))
             fwd_copy(micro).start()
+
+            @pl.when(leads & (micro == 0))
+            def _():
+                fwd_copy(micro).wait_send()
+                pl.semaphore_signal(token, inc=1, device_id=sibling, device_id_type=MESH)
 
         units[micro] = unit.astype(BF16)
         stats[micro, :, 2:3] = inverse
@@ -888,7 +908,7 @@
             pltpu.VMEM((3, 16, WIDTH), F32),
             dma((12,)), dma, dma((2,)), dma, dma((4, 2)),
             dma((SLOTS,)), dma((SLOTS,)), dma((SLOTS,)), dma((SLOTS,)),
-            dma((SLOTS, 4)), dma((SLOTS,)),
+            dma((SLOTS, 4)), dma((SLOTS,)), pltpu.SemaphoreType.REGULAR,
             dma, dma((2,)), pltpu.SemaphoreType.REGULAR,
             dma((2,)), dma((8, CHUNKS)), dma, dma((2, 2)), dma, dma, dma((CHUNKS,)), dma, dma,
             dma((12,)), dma((12,)),
@@ -955,7 +975,7 @@
 
 def widen(reduced, sums, grad):
     any_space = pl.BlockSpec(memory_space=pl.ANY)
-    rows, depth = 512, 4
+    rows, depth = 1024, 3
     dma = pltpu.SemaphoreType.DMA
     shapes = [(2, 2, WIDTH), (2, FF), (1, WIDTH), (1, 2, WIDTH), (1, 2, WIDTH)]
     return pl.pallas_call(

time: 195 us -> 190 us (0.974)
  Pallas kernels: 192 us -> 186 us
    pallas_call x1, Pallas kernels: 180 us -> 174 us  [mega(): pl.pallas_call(mega_kernel, name='mega', out_shape=[jax.ShapeDtypeStruct(...]
where the time goes in v5:
time: 190 us; the launch traced here: 188 us
  Pallas kernels  186 us (98%)
    pallas_call x1, Pallas kernels, mega(): pl.pallas_call(mega_kernel, name='mega', out_shape=[jax.ShapeDtypeStruct(...  174 us
    pallas_call x1, Pallas kernels, widen(): pl.pallas_call(widen_kernel, name='widen', out_shape=[jax.ShapeDtypeStruc...  12 us

profile of v5, /device:TPU:33, one launch (start us, length us, event | category | flops | bytes accessed | tf_op | source)
XLA Modules:
  0.0 187.5 jit_solution(7411731506689129934)
XLA Ops:
  1.3 174.1 %mega.1 = (bf16[6144,1024]{1,0:T(8,128)(2,1)}, f32[5,16,1024]{2,1,0:T(8,128)}, bf16[4,128,256]{2,1,0:T(8,128)(2,1)}) custom-call(bf16[4,128,1024]{2,1,0:T(8,128)(2,1)} %block_hbm.1, bf16[4,128,1024]{2,1,0:T(8,128)(2,1)} %cot_hbm.1, s32[4]{0:T(128)} %group_hbm.1, s32[1]{0:T(128)S(6)} %copy.20.live_hbm, f32[8]{0:T(128)} %scale_hbm.1, f32[1,2,1024]{2,1,0:T(2,128)} %gains_hbm.1, ...), custom_call_target="tpu_custom_call" | custom-call | tf_op jit(solution)/shard_map/mega/pallas_call | solution.py:871
  175.3 12.0 %widen.1 = (f32[1,1024,4096]{2,1,0:T(8,128)}, f32[2048,1024]{1,0:T(8,128)}, f32[2,2,1024]{2,1,0:T(2,128)}, f32[2,4096]{1,0:T(2,128)}, f32[1,1024]{1,0:T(1,128)},...) custom-call(bf16[6144,1024]{1,0:T(8,128)(2,1)} %get-tuple-element.19.reduced, ...), custom_call_target="tpu_custom_call" | custom-call | tf_op jit(solution)/shard_map/widen/pallas_call | solution.py:981

commit v6 on v5

--- a/solution.py
+++ b/solution.py
@@ -35,21 +35,26 @@
     return lax.axis_index("section"), at // 8, (at // 2) % 4, at % 2
 
 
-def neighbours(section, x, y, core):
-    found = [device(section, x, y, 1 - core)]
+def greet(section, x, y, core, here):
+    barrier = pltpu.get_barrier_semaphore()
+    others = [device(section, x, y, 1 - core), device(section + 1 - 2 * (section % 2), x, y, core)]
     for d in (1, 2, 3):
-        found.append(device(section, (x + d) % 4, y, core))
-        found.append(device(section, x, (y + d) % 4, core))
-        found.append(device((section + d) % 4, x, y, core))
-    return found
-
-
-def greet(section, x, y, core):
-    barrier = pltpu.get_barrier_semaphore()
-    others = neighbours(section, x, y, core)
+        others.append(device(section, (x + d) % 4, y, core))
+        others.append(device(section, x, (y + d) % 4, core))
     for other in others:
         pl.semaphore_signal(barrier, inc=1, device_id=other, device_id_type=MESH)
-    pl.semaphore_wait(barrier, len(others))
+
+    @pl.when(section < 2)
+    def _():
+        for high in (2, 3):
+            pl.semaphore_signal(barrier, inc=1, device_id=device(high, x, y, core), device_id_type=MESH)
+
+    pl.semaphore_wait(barrier, jnp.where(section < 2, 8, 10))
+
+    @pl.when(section >= 2)
+    def _():
+        for low in (0, 1):
+            pl.semaphore_signal(here, inc=1, device_id=device(low, x, y, core), device_id_type=MESH)
 
 
 def remote(source, target, send_sem, recv_sem, to):
@@ -100,7 +105,7 @@
     w1, buffer, w2t, ops, other, units, stats, r_in, r_out, g_in, g_out, wide, small, vectors,
     z, sx, sy, ss, sums,
     load_sem, down_send, down_recv, ag_send, ag_recv,
-    fwd_send, fwd_recv, bwd_send, bwd_recv, ig_send, ig_recv, token,
+    fwd_send, fwd_recv, bwd_send, bwd_recv, ig_send, ig_recv, token, here,
     swap_send, swap_recv, ready, ring_send, ring_recv, z_send, z_recv, export_send, export_recv, own_sem, last_send, last_recv,
     tiny_send, tiny_recv,
 ):
@@ -139,7 +144,7 @@
     def _():
         load_cot.start()
 
-    greet(section, x, y, core)
+    greet(section, x, y, core, here)
 
     left, right = pl.ds(0, 512), pl.ds(512, 512)
     both = [(h, d) for h in (0, 1) for d in (0, 1)]
@@ -427,6 +432,7 @@
             leads = (section == 1) & (core == 1)
             follows = (section == 1) & (core == 0)
             pl.when(micro > jnp.where(leads, 1, 0))(lambda: fwd_copy(micro - 1).wait_send())
+            pl.when((section < 2) & (micro == 0))(lambda: pl.semaphore_wait(here, 2))
             pl.when(follows & (micro == 0))(lambda: pl.semaphore_wait(token, 1))
             fwd_copy(micro).start()
 
@@ -908,7 +914,7 @@
             pltpu.VMEM((3, 16, WIDTH), F32),
             dma((12,)), dma, dma((2,)), dma, dma((4, 2)),
             dma((SLOTS,)), dma((SLOTS,)), dma((SLOTS,)), dma((SLOTS,)),
-            dma((SLOTS, 4)), dma((SLOTS,)), pltpu.SemaphoreType.REGULAR,
+            dma((SLOTS, 4)), dma((SLOTS,)), pltpu.SemaphoreType.REGULAR, pltpu.SemaphoreType.REGULAR,
             dma, dma((2,)), pltpu.SemaphoreType.REGULAR,
             dma((2,)), dma((8, CHUNKS)), dma, dma((2, 2)), dma, dma, dma((CHUNKS,)), dma, dma,
             dma((12,)), dma((12,)),

time: 190 us -> 187 us (0.984)
  Pallas kernels: 186 us -> 184 us
    pallas_call x1, Pallas kernels: 174 us -> 172 us  [mega(): pl.pallas_call(mega_kernel, name='mega', out_shape=[jax.ShapeDtypeStruct(...]
where the time goes in v6:
time: 187 us; the launch traced here: 185 us
  Pallas kernels  184 us (98%)
    pallas_call x1, Pallas kernels, mega(): pl.pallas_call(mega_kernel, name='mega', out_shape=[jax.ShapeDtypeStruct(...  172 us
    pallas_call x1, Pallas kernels, widen(): pl.pallas_call(widen_kernel, name='widen', out_shape=[jax.ShapeDtypeStruc...  12 us

profile of v6, /device:TPU:33, one launch (start us, length us, event | category | flops | bytes accessed | tf_op | source)
XLA Modules:
  0.0 185.4 jit_solution(1752301142100131690)
XLA Ops:
  1.3 171.9 %mega.1 = (bf16[6144,1024]{1,0:T(8,128)(2,1)}, f32[5,16,1024]{2,1,0:T(8,128)}, bf16[4,128,256]{2,1,0:T(8,128)(2,1)}) custom-call(bf16[4,128,1024]{2,1,0:T(8,128)(2,1)} %block_hbm.1, bf16[4,128,1024]{2,1,0:T(8,128)(2,1)} %cot_hbm.1, s32[4]{0:T(128)} %group_hbm.1, s32[1]{0:T(128)S(6)} %copy.20.live_hbm, f32[8]{0:T(128)} %scale_hbm.1, f32[1,2,1024]{2,1,0:T(2,128)} %gains_hbm.1, ...), custom_call_target="tpu_custom_call" | custom-call | tf_op jit(solution)/shard_map/mega/pallas_call | solution.py:877
  173.2 12.0 %widen.1 = (f32[1,1024,4096]{2,1,0:T(8,128)}, f32[2048,1024]{1,0:T(8,128)}, f32[2,2,1024]{2,1,0:T(2,128)}, f32[2,4096]{1,0:T(2,128)}, f32[1,1024]{1,0:T(1,128)},...) custom-call(bf16[6144,1024]{1,0:T(8,128)(2,1)} %get-tuple-element.19.reduced, ...), custom_call_target="tpu_custom_call" | custom-call | tf_op jit(solution)/shard_map/widen/pallas_call | solution.py:987

commit v7 on v6

--- a/solution.py
+++ b/solution.py
@@ -49,12 +49,15 @@
         for high in (2, 3):
             pl.semaphore_signal(barrier, inc=1, device_id=device(high, x, y, core), device_id_type=MESH)
 
-    pl.semaphore_wait(barrier, jnp.where(section < 2, 8, 10))
-
-    @pl.when(section >= 2)
-    def _():
-        for low in (0, 1):
-            pl.semaphore_signal(here, inc=1, device_id=device(low, x, y, core), device_id_type=MESH)
+    def wait():
+        pl.semaphore_wait(barrier, jnp.where(section < 2, 8, 10))
+
+        @pl.when(section >= 2)
+        def _():
+            for low in (0, 1):
+                pl.semaphore_signal(here, inc=1, device_id=device(low, x, y, core), device_id_type=MESH)
+
+    return wait
 
 
 def remote(source, target, send_sem, recv_sem, to):
@@ -117,6 +120,7 @@
     sibling = device(section, x, y, 1 - core)
     w1t, w2 = buffer.at[pl.ds(0, FF)], buffer.at[pl.ds(FF, FF)]
 
+    meet = greet(section, x, y, core, here)
     load_w1 = pltpu.make_async_copy(w1_hbm.at[0], w1, load_sem.at[0])
     load_own = pltpu.make_async_copy(down_hbm, w2.at[pl.ds(2048, 2048)], load_sem.at[1])
     load_block = pltpu.make_async_copy(block_hbm, r_in, load_sem.at[2])
@@ -144,7 +148,7 @@
     def _():
         load_cot.start()
 
-    greet(section, x, y, core, here)
+    meet()
 
     left, right = pl.ds(0, 512), pl.ds(512, 512)
     both = [(h, d) for h in (0, 1) for d in (0, 1)]
@@ -329,7 +333,14 @@
                 ops[3 + p // 4, micro, :, (p % 4 * 2 + head) * 128 : (p % 4 * 2 + head + 1) * 128] = part
                 parts.append(part)
             ops[2, micro, :, cut] = dot_tn(jnp.concatenate(parts, axis=0), two_heads(value)).astype(BF16)
-        wide[...] = dot_nt(ops[2, micro], w1[:, 3 * WIDTH :]) + out_bias[...]
+
+        @pl.when(section == 2)
+        def _():
+            wide[...] = dot(ops[2, micro], w1t[3 * WIDTH :, :]) + out_bias[...]
+
+        @pl.when(section != 2)
+        def _():
+            wide[...] = dot_nt(ops[2, micro], w1[:, 3 * WIDTH :]) + out_bias[...]
 
     def feed_forward(micro):
         normed = ops[0, micro]
@@ -413,7 +424,7 @@
         stats[micro, :, 0:1] = mean
         stats[micro, :, 1:2] = inverse
         ops[0, micro] = (centered * inverse * gains[0, 0:1, :] + shifts[0, 0:1, :]).astype(BF16)
-        swap(0, 1, micro, 0).start()
+        pl.when(jnp.logical_not(last))(lambda: swap(0, 1, micro, 0).start())
 
         @pl.when(parity == 0)
         def _():
@@ -444,7 +455,7 @@
         units[micro] = unit.astype(BF16)
         stats[micro, :, 2:3] = inverse
         pl.when(parity == 0)(lambda: swap(2, 1, micro, 0).start())
-        pl.when(parity == 1)(lambda: swap(2, 4, micro, 0).start())
+        pl.when(section == 1)(lambda: swap(2, 4, micro, 0).start())
 
     def backward(micro):
         @pl.when(jnp.logical_not(last))
@@ -455,7 +466,7 @@
         incoming = g_in[micro].astype(F32) * weight
         unit = units[micro].astype(F32)
         ops[1, micro] = norm_backward(incoming, unit, stats[micro, :, 2:3], gains[0, 1:2, :]).astype(BF16)
-        swap(1, 1, micro, 0).start()
+        pl.when(jnp.logical_not(last))(lambda: swap(1, 1, micro, 0).start())
 
         @pl.when(parity == 0)
         def _():
@@ -483,7 +494,7 @@
 
         r_out[micro] = wide[...].astype(BF16)
         pl.when(parity == 0)(lambda: swap(6, 3, micro, 1).start())
-        pl.when(parity == 1)(lambda: swap(6, 4, micro, 1).start())
+        pl.when(section == 1)(lambda: swap(6, 4, micro, 1).start())
 
     def row_sums(micro):
         weight = sequence_weight(micro)
@@ -524,6 +535,12 @@
 
     lax.fori_loop(0, 2 * SLOTS, step, 0)
 
+    @pl.when(last)
+    def _():
+        for block, count, group in ((0, 6, 0), (6, 4, 1)):
+            piece = pl.ds(block, count)
+            remote(ops.at[piece], other.at[piece], swap_send, swap_recv.at[group], sibling).start()
+
     def spot(h):
         return (x, y) if h == 0 else (y, x)
 
@@ -531,14 +548,14 @@
     takes_in = section == 2
 
     def chunk(q):
-        late = jnp.where(takes_in, jnp.where(q == 7, 2, q - 4), jnp.where(q == 4, 1, 0))
+        late = jnp.where(takes_in, jnp.where(q == 6, 2, q - 4), jnp.where(q == 4, 1, 0))
         return jnp.where(parity == 1, q, jnp.where(q < 4, 7 - q, late))
 
     def exported(q):
         return sends_out & (q == 0)
 
     def imported(q):
-        return takes_in & (q == 7)
+        return takes_in & (q == 6)
 
     def multiplies(q):
         return (parity == 1) | (q < 4)

time: 187 us -> 185 us (0.989)
  no operation moved by 1% of the time
where the time goes in v7:
time: 185 us
  Pallas kernels  184 us (99%)
    pallas_call x1, Pallas kernels, mega(): pl.pallas_call(mega_kernel, name='mega', out_shape=[jax.ShapeDtypeStruct(...  172 us
    pallas_call x1, Pallas kernels, widen(): pl.pallas_call(widen_kernel, name='widen', out_shape=[jax.ShapeDtypeStruc...  12 us

profile of v7, /device:TPU:33, one launch (start us, length us, event | category | flops | bytes accessed | tf_op | source)
XLA Modules:
  0.0 185.2 jit_solution(13035768797508334251)
XLA Ops:
  1.3 171.7 %mega.1 = (bf16[6144,1024]{1,0:T(8,128)(2,1)}, f32[5,16,1024]{2,1,0:T(8,128)}, bf16[4,128,256]{2,1,0:T(8,128)(2,1)}) custom-call(bf16[4,128,1024]{2,1,0:T(8,128)(2,1)} %block_hbm.1, bf16[4,128,1024]{2,1,0:T(8,128)(2,1)} %cot_hbm.1, s32[4]{0:T(128)} %group_hbm.1, s32[1]{0:T(128)S(6)} %copy.20.live_hbm, f32[8]{0:T(128)} %scale_hbm.1, f32[1,2,1024]{2,1,0:T(2,128)} %gains_hbm.1, ...), custom_call_target="tpu_custom_call" | custom-call | tf_op jit(solution)/shard_map/mega/pallas_call | solution.py:894
  173.0 12.0 %widen.1 = (f32[1,1024,4096]{2,1,0:T(8,128)}, f32[2048,1024]{1,0:T(8,128)}, f32[2,2,1024]{2,1,0:T(2,128)}, f32[2,4096]{1,0:T(2,128)}, f32[1,1024]{1,0:T(1,128)},...) custom-call(bf16[6144,1024]{1,0:T(8,128)(2,1)} %get-tuple-element.19.reduced, ...), custom_call_target="tpu_custom_call" | custom-call | tf_op jit(solution)/shard_map/widen/pallas_call | solution.py:1004

commit v8 on v7

--- a/solution.py
+++ b/solution.py
@@ -832,9 +832,8 @@
             pl.semaphore_signal(ready, inc=1, device_id=peer(axis, d), device_id_type=MESH)
 
     def slot(t, carry):
-        pl.when((t >= 3) & (t < 3 + SLOTS))(lambda: row_sums(t - 3))
         for number, turn in enumerate((tiny_0, tiny_1, tiny_2, tiny_3)):
-            pl.when(t == 3 + SLOTS + number)(turn)
+            pl.when(t == 2 + SLOTS + number)(turn)
         for s in ORDER:
             k = t - jnp.where(parity == 1, OFFSET_FEED[s], OFFSET_ATTEND[s])
             live = (k >= 0) & (k < CHUNKS)
@@ -847,6 +846,7 @@
             else:
                 live = live & gathers(k)
             pl.when(live)(lambda turn=stages[s], k=k: turn(k))
+        pl.when((t >= 1) & (t < 1 + SLOTS))(lambda: row_sums(t - 1))
         return carry
 
     lax.fori_loop(0, CHUNKS + max(OFFSET_FEED + OFFSET_ATTEND), slot, 0)

time: 185 us -> 187 us (1.011)
  no operation moved by 1% of the time
where the time goes in v8:
time: 187 us
  Pallas kernels  185 us (99%)
    pallas_call x1, Pallas kernels, mega(): pl.pallas_call(mega_kernel, name='mega', out_shape=[jax.ShapeDtypeStruct(...  173 us
    pallas_call x1, Pallas kernels, widen(): pl.pallas_call(widen_kernel, name='widen', out_shape=[jax.ShapeDtypeStruc...  12 us

profile of v8, /device:TPU:33, one launch (start us, length us, event | category | flops | bytes accessed | tf_op | source)
XLA Modules:
  0.0 186.6 jit_solution(16023851569785580627)
XLA Ops:
  1.3 173.1 %mega.1 = (bf16[6144,1024]{1,0:T(8,128)(2,1)}, f32[5,16,1024]{2,1,0:T(8,128)}, bf16[4,128,256]{2,1,0:T(8,128)(2,1)}) custom-call(bf16[4,128,1024]{2,1,0:T(8,128)(2,1)} %block_hbm.1, bf16[4,128,1024]{2,1,0:T(8,128)(2,1)} %cot_hbm.1, s32[4]{0:T(128)} %group_hbm.1, s32[1]{0:T(128)S(6)} %copy.20.live_hbm, f32[8]{0:T(128)} %scale_hbm.1, f32[1,2,1024]{2,1,0:T(2,128)} %gains_hbm.1, ...), custom_call_target="tpu_custom_call" | custom-call | tf_op jit(solution)/shard_map/mega/pallas_call | solution.py:894
  174.4 12.0 %widen.1 = (f32[1,1024,4096]{2,1,0:T(8,128)}, f32[2048,1024]{1,0:T(8,128)}, f32[2,2,1024]{2,1,0:T(2,128)}, f32[2,4096]{1,0:T(2,128)}, f32[1,1024]{1,0:T(1,128)},...) custom-call(bf16[6144,1024]{1,0:T(8,128)(2,1)} %get-tuple-element.19.reduced, ...), custom_call_target="tpu_custom_call" | custom-call | tf_op jit(solution)/shard_map/widen/pallas_call | solution.py:1004
